TPU v7x, 32 devices: a whole 2x2x4 slice. The times are simulated.
32 devices in a mesh: section: 4 (over y, x), dp: 8 (over z, core).
Axes of the slice: x: 2, y: 2, z: 4, core: 2. Of those that a mesh axis runs over, the one named last changes fastest.
Arguments:
- inputs: bfloat16 [8, 2, 502, 768], P('dp', None, None, 'section'), may hold values from -6 to 6
- out_grad: bfloat16 [8, 2, 502, 768], P('dp', None, None, 'section'), may hold values from -6 to 6
- memory: bfloat16 [8, 10, 768], P('dp', None, 'section'), may hold values from -6 to 6
- lengths: int32 [8], P('dp'), may hold values from 251 to 1004, as said below
- w_qkv: bfloat16 [4, 768, 2304], P('section'), may hold values from -0.21875 to 0.21875
- w_proj: bfloat16 [4, 768, 768], P('section'), may hold values from -3 to 3
- gain_one: float32 [4, 768], P('section'), may hold values from 0.1 to 1.9
- shift_one: float32 [4, 768], P('section'), may hold values from -3 to 3
- w_in: bfloat16 [4, 768, 3072], P('section'), may hold values from -0.21875 to 0.21875
- b_in: float32 [4, 3072], P('section'), may hold values from -3 to 3
- w_down: bfloat16 [4, 3072, 768], P('section'), may hold values from -0.109375 to 0.109375
- gain_two: float32 [4, 768], P('section'), may hold values from 0.1 to 1.9
- shift_two: float32 [4, 768], P('section'), may hold values from -3 to 3
Outputs:
- outputs: bfloat16 [8, 2, 502, 768], P('dp', None, None, 'section')
- input_grad: bfloat16 [8, 2, 502, 768], P('dp', None, None, 'section')
- memory_grad: float32 [8, 10, 768], P('dp', None, 'section')
- grad_w_qkv: float32 [4, 768, 2304], P('section', 'dp')
- grad_w_proj: float32 [4, 768, 768], P('section', 'dp')
- grad_gain_one: float32 [4, 768], P('section', 'dp')
- grad_shift_one: float32 [4, 768], P('section', 'dp')
- grad_w_in: float32 [4, 768, 3072], P('section', 'dp')
- grad_b_in: float32 [4, 3072], P('section', 'dp')
- grad_w_down: float32 [4, 3072, 768], P('section', 'dp')
- grad_gain_two: float32 [4, 768], P('section', 'dp')
- grad_shift_two: float32 [4, 768], P('section', 'dp')
Inputs may be any that keep to these rules, and one draw needn't show every extreme that they name: `lengths`: an item's tokens fill its segments in order; one item of the batch has exactly 1004 tokens.
All inputs are finite; a program needn't handle non-finite values.
Results may differ from a plain program's by a relative error of at most 0.018.
Values may be sent and summed in bfloat16 or wider, within the bound.
A program may use at most 320 MiB of HBM per device.

v0:
```python
import jax
import jax.numpy as jnp
from jax import lax
from jax.sharding import PartitionSpec as P

D = 768
H = 12
HEAD = 64
FF = 3072


def shifted(value, axis, by):
    devices = lax.axis_size(axis)
    return lax.ppermute(value, axis, [(i, (i + by) % devices) for i in range(devices)])


def layer_norm(summed, norm_gain, norm_shift):
    center = summed - jnp.mean(summed, axis=-1, keepdims=True)
    spread = jnp.mean(center * center, axis=-1, keepdims=True)
    return center * lax.rsqrt(spread + 1e-06) * norm_gain + norm_shift


def gelu_exact(value_in):
    return jax.nn.gelu(value_in, approximate=False)


def key_masks(length, segment, tok_rows, mem_rows):
    position = segment * tok_rows + jnp.arange(tok_rows, dtype=jnp.int32)
    token_valid = (position < length)[None, :]
    memory_edge = jnp.ones((1, mem_rows), dtype=bool)
    return (
        jnp.concatenate([memory_edge, token_valid, memory_edge], axis=1),
        token_valid.astype(jnp.float32),
    )


def clock_slot(tick_index, offset, period, num_items, segs):
    offset_place = tick_index - offset
    seg_group = jnp.floor_divide(offset_place, period)
    within = offset_place - seg_group * period
    is_live = (offset_place >= 0) & (within < num_items) & (seg_group < segs)
    item_slot = jnp.clip(within, 0, num_items - 1).astype(jnp.int32)
    seg_slot = jnp.clip(seg_group, 0, segs - 1).astype(jnp.int32)
    return (is_live, item_slot, seg_slot)


def split_heads(projected):
    pieces = projected.reshape(projected.shape[0], projected.shape[1], 3, H, HEAD)
    return (pieces[:, :, 0], pieces[:, :, 1], pieces[:, :, 2])


def score_block(queries, keys, key_valid):
    scores = jnp.einsum(
        "bqhc,bkhc->bhqk", queries, keys, preferred_element_type=jnp.float32
    ) * HEAD ** (-0.5)
    return jnp.where(key_valid[:, None, None, :], scores, -1e30)


def attention_forward(projected, key_valid):
    queries, keys, values = split_heads(projected)
    scores = score_block(queries, keys, key_valid)
    row_max = jnp.max(scores, axis=-1, keepdims=True)
    exponent = jnp.exp(scores - row_max)
    denominator = jnp.sum(exponent, axis=-1, keepdims=True)
    attn_probs = (exponent / denominator).astype(jnp.bfloat16)
    mixed_heads = jnp.einsum(
        "bhqk,bkhc->bqhc", attn_probs, values, preferred_element_type=jnp.float32
    )
    attended = mixed_heads.reshape(projected.shape[0], projected.shape[1], D).astype(jnp.bfloat16)
    return (attended, (row_max + jnp.log(denominator))[..., 0])


def attention_backward(projected, key_valid, log_total, grad_attended):
    queries, keys, values = split_heads(projected)
    scores = score_block(queries, keys, key_valid)
    probs_full = jnp.exp(scores - log_total[..., None])
    grad_heads = grad_attended.reshape(projected.shape[0], projected.shape[1], H, HEAD)
    grad_values = jnp.einsum(
        "bhqk,bqhc->bkhc",
        probs_full.astype(jnp.bfloat16),
        grad_heads,
        preferred_element_type=jnp.float32,
    )
    grad_probs = jnp.einsum(
        "bqhc,bkhc->bhqk", grad_heads, values, preferred_element_type=jnp.float32
    )
    row_term = jnp.sum(probs_full * grad_probs, axis=-1, keepdims=True)
    grad_scores = (probs_full * (grad_probs - row_term)).astype(jnp.bfloat16)
    grad_queries = jnp.einsum(
        "bhqk,bkhc->bqhc", grad_scores, keys, preferred_element_type=jnp.float32
    ) * HEAD ** (-0.5)
    grad_keys = jnp.einsum(
        "bhqk,bqhc->bkhc", grad_scores, queries, preferred_element_type=jnp.float32
    ) * HEAD ** (-0.5)
    stacked = jnp.stack([grad_queries, grad_keys, grad_values], axis=2)
    return stacked.reshape(projected.shape[0], projected.shape[1], 3 * D).astype(jnp.bfloat16)


def layer_forward(hidden, key_valid, params):
    w_qkv, w_proj, gain_one, shift_one, w_in, b_in, w_down, gain_two, shift_two = params
    projected = jnp.einsum(
        "brd,de->bre", hidden.astype(jnp.bfloat16), w_qkv, preferred_element_type=jnp.float32
    ).astype(jnp.bfloat16)
    attended, log_total = attention_forward(projected, key_valid)
    first_sum = hidden + jnp.einsum(
        "brd,de->bre", attended, w_proj, preferred_element_type=jnp.float32
    )
    normed = layer_norm(first_sum, gain_one, shift_one)
    pre_act = (
        jnp.einsum(
            "brd,df->brf", normed.astype(jnp.bfloat16), w_in, preferred_element_type=jnp.float32
        )
        + b_in
    )
    activated = gelu_exact(pre_act).astype(jnp.bfloat16)
    second_sum = normed + jnp.einsum(
        "brf,fd->brd", activated, w_down, preferred_element_type=jnp.float32
    )
    kept_data = (hidden, projected, log_total, attended, first_sum, pre_act, second_sum)
    return (layer_norm(second_sum, gain_two, shift_two), kept_data)


def layer_backward(grad_out, key_valid, params, kept_data):
    w_qkv, w_proj, gain_one, shift_one, w_in, b_in, w_down, gain_two, shift_two = params
    hidden, projected, log_total, attended, first_sum, pre_act, second_sum = kept_data
    normed = layer_norm(first_sum, gain_one, shift_one)
    unused_two, pull_two = jax.vjp(layer_norm, second_sum, gain_two, shift_two)
    grad_second, grad_gain_two, grad_shift_two = pull_two(grad_out)
    grad_feed = grad_second.astype(jnp.bfloat16)
    activated = gelu_exact(pre_act).astype(jnp.bfloat16)
    grad_w_down = jnp.einsum(
        "brf,brd->fd", activated, grad_feed, preferred_element_type=jnp.float32
    )
    grad_act = jnp.einsum("brd,fd->brf", grad_feed, w_down, preferred_element_type=jnp.float32)
    unused_gelu, pull_gelu = jax.vjp(gelu_exact, pre_act)
    grad_pre = pull_gelu(grad_act)[0].astype(jnp.bfloat16)
    grad_b_in = jnp.sum(grad_pre.astype(jnp.float32), axis=(0, 1))
    grad_w_in = jnp.einsum(
        "brd,brf->df", normed.astype(jnp.bfloat16), grad_pre, preferred_element_type=jnp.float32
    )
    grad_normed = grad_second + jnp.einsum(
        "brf,df->brd", grad_pre, w_in, preferred_element_type=jnp.float32
    )
    unused_one, pull_one = jax.vjp(layer_norm, first_sum, gain_one, shift_one)
    grad_first, grad_gain_one, grad_shift_one = pull_one(grad_normed)
    grad_branch = grad_first.astype(jnp.bfloat16)
    grad_w_proj = jnp.einsum(
        "brd,bre->de", attended, grad_branch, preferred_element_type=jnp.float32
    )
    grad_attended = jnp.einsum(
        "bre,de->brd", grad_branch, w_proj, preferred_element_type=jnp.float32
    ).astype(jnp.bfloat16)
    grad_projected = attention_backward(projected, key_valid, log_total, grad_attended)
    grad_w_qkv = jnp.einsum(
        "brd,bre->de",
        hidden.astype(jnp.bfloat16),
        grad_projected,
        preferred_element_type=jnp.float32,
    )
    grad_hidden = grad_first + jnp.einsum(
        "bre,de->brd", grad_projected, w_qkv, preferred_element_type=jnp.float32
    )
    layer_grads = (
        grad_w_qkv,
        grad_w_proj,
        grad_gain_one,
        grad_shift_one,
        grad_w_in,
        grad_b_in,
        grad_w_down,
        grad_gain_two,
        grad_shift_two,
    )
    return (grad_hidden, layer_grads)


def section_forward(rows_in, key_valid, section_params):
    hidden = rows_in.astype(jnp.float32)
    hidden, kept_data = layer_forward(hidden, key_valid, section_params[0])
    kept_all = [kept_data]
    return (hidden.astype(jnp.bfloat16), tuple(kept_all))


def section_backward(grad_rows, key_valid, section_params, kept_all, grad_sums):
    grad_hidden = grad_rows
    new_sums = list(grad_sums)
    for layer_index in reversed(range(len(section_params))):
        grad_hidden, layer_grads = layer_backward(
            grad_hidden, key_valid, section_params[layer_index], kept_all[layer_index]
        )
        new_sums[layer_index] = tuple(
            (
                total_part + new_part
                for total_part, new_part in zip(new_sums[layer_index], layer_grads)
            )
        )
        grad_hidden = grad_hidden.astype(jnp.bfloat16).astype(jnp.float32)
    return (grad_hidden.astype(jnp.bfloat16), tuple(new_sums))


def blank_kept(count, num_rows, layer_count):
    one_layer = (
        jnp.zeros((count, 1, num_rows, D), jnp.float32),
        jnp.zeros((count, 1, num_rows, 3 * D), jnp.bfloat16),
        jnp.zeros((count, 1, H, num_rows), jnp.float32),
        jnp.zeros((count, 1, num_rows, D), jnp.bfloat16),
        jnp.zeros((count, 1, num_rows, D), jnp.float32),
        jnp.zeros((count, 1, num_rows, FF), jnp.float32),
        jnp.zeros((count, 1, num_rows, D), jnp.float32),
    )
    return tuple([one_layer] * layer_count)


def blank_grads(section_params):
    return tuple(
        (
            tuple((jnp.zeros(weight.shape, jnp.float32) for weight in layer_params))
            for layer_params in section_params
        )
    )


def stack_grads(grad_sums):
    return tuple((jnp.stack(bundle) for bundle in zip(*grad_sums)))


def on_device(
    inputs,
    out_grad,
    memory,
    lengths,
    w_qkv,
    w_proj,
    gain_one,
    shift_one,
    w_in,
    b_in,
    w_down,
    gain_two,
    shift_two,
):
    sections = lax.axis_size("section")
    section_id = lax.axis_index("section")
    weights = (w_qkv, w_proj, gain_one, shift_one, w_in, b_in, w_down, gain_two, shift_two)
    layer_count = w_qkv.shape[0]
    section_params = tuple(
        (tuple((weight[layer_index] for weight in weights)) for layer_index in range(layer_count))
    )
    num_items, segs, tok_rows = (inputs.shape[0], inputs.shape[1], inputs.shape[2])
    mem_rows = memory.shape[1]
    num_rows = 2 * mem_rows + tok_rows
    full_tokens, full_cotangent, full_memory = (
        lax.all_gather(inputs, "section", axis=3, tiled=True),
        lax.all_gather(out_grad, "section", axis=3, tiled=True),
        lax.all_gather(memory[:, None], "section", axis=3, tiled=True),
    )
    period = max(num_items, sections)
    clocks = (segs - 1) * period + num_items - 1 + sections
    memory_store = full_memory[:, 0]
    received = jnp.zeros((1, num_rows, D), jnp.bfloat16)
    kept_store = blank_kept(num_items * segs, num_rows, layer_count)
    out_store = jnp.zeros((num_items, segs, tok_rows, D), jnp.float32)
    for tick_index in range(clocks):
        arrive_live, arrive_item, arrive_seg = clock_slot(
            tick_index, sections, period, num_items, segs
        )
        held = lax.dynamic_index_in_dim(memory_store, arrive_item, 0, keepdims=False)
        incoming = jnp.where(arrive_live, received[0, mem_rows + tok_rows :], held)
        memory_store = lax.dynamic_update_index_in_dim(memory_store, incoming, arrive_item, 0)
        is_live, item_slot, seg_slot = clock_slot(tick_index, section_id, period, num_items, segs)
        length = lax.dynamic_index_in_dim(lengths, item_slot, 0, keepdims=False)
        key_valid, token_valid = key_masks(length, seg_slot, tok_rows, mem_rows)
        memory_rows = lax.dynamic_index_in_dim(memory_store, item_slot, 0, keepdims=True)
        token_rows = lax.dynamic_slice(
            full_tokens, (item_slot, seg_slot, 0, 0), (1, 1, tok_rows, D)
        )[:, 0]
        composed = jnp.concatenate([memory_rows, token_rows, memory_rows], axis=1)
        rows_in = jnp.where(section_id == 0, composed, received)
        flat_slot = item_slot * segs + seg_slot

        def run_section(rows_in, kept_store, out_store):
            rows_out, kept_now = section_forward(rows_in, key_valid, section_params)
            kept_store = jax.tree.map(
                lambda buffer, fresh: lax.dynamic_update_index_in_dim(buffer, fresh, flat_slot, 0),
                kept_store,
                kept_now,
            )
            token_out = (
                rows_out[:, mem_rows : mem_rows + tok_rows].astype(jnp.float32)
                * token_valid[:, :, None]
            )
            out_store = lax.dynamic_update_slice(
                out_store, token_out[:, None], (item_slot, seg_slot, 0, 0)
            )
            return (rows_out, kept_store, out_store)

        def pass_section(rows_in, kept_store, out_store):
            return (rows_in, kept_store, out_store)

        rows_out, kept_store, out_store = lax.cond(
            is_live, run_section, pass_section, rows_in, kept_store, out_store
        )
        received = shifted(rows_out, "section", 1)

    def back_tick(tick_index, carry):
        grad_store, grad_received, grad_sums, in_store, memory_out = carry
        arrive_live, arrive_back, unused_seg = clock_slot(
            tick_index, sections, period, num_items, segs
        )
        arrive_item = num_items - 1 - arrive_back
        held = lax.dynamic_index_in_dim(grad_store, arrive_item, 0, keepdims=False)
        incoming = grad_received[0, :mem_rows].astype(jnp.float32) + grad_received[
            0, mem_rows + tok_rows :
        ].astype(jnp.float32)
        grad_store = lax.dynamic_update_index_in_dim(
            grad_store, jnp.where(arrive_live, incoming, held), arrive_item, 0
        )
        is_live, back_item, back_seg = clock_slot(
            tick_index, sections - 1 - section_id, period, num_items, segs
        )
        item_slot = num_items - 1 - back_item
        seg_slot = segs - 1 - back_seg
        length = lax.dynamic_index_in_dim(lengths, item_slot, 0, keepdims=False)
        key_valid, token_valid = key_masks(length, seg_slot, tok_rows, mem_rows)
        carried = jnp.where(
            seg_slot == segs - 1,
            0.0,
            lax.dynamic_index_in_dim(grad_store, item_slot, 0, keepdims=True),
        )
        cotangent = lax.dynamic_slice(
            full_cotangent, (item_slot, seg_slot, 0, 0), (1, 1, tok_rows, D)
        )[:, 0]
        token_grad = cotangent.astype(jnp.float32) * token_valid[:, :, None]
        grad_seed = jnp.concatenate(
            [jnp.zeros((1, mem_rows, D), jnp.float32), token_grad, carried], axis=1
        )
        grad_in = jnp.where(
            section_id == sections - 1, grad_seed, grad_received.astype(jnp.float32)
        )
        flat_slot = item_slot * segs + seg_slot

        def run_back(grad_in, grad_sums, in_store, memory_out):
            kept_now = jax.tree.map(
                lambda buffer: lax.dynamic_index_in_dim(buffer, flat_slot, 0, keepdims=False),
                kept_store,
            )
            grad_rows, grad_sums = section_backward(
                grad_in, key_valid, section_params, kept_now, grad_sums
            )
            token_part = grad_rows[:, mem_rows : mem_rows + tok_rows].astype(jnp.float32)
            in_store = lax.dynamic_update_slice(
                in_store, token_part[:, None], (item_slot, seg_slot, 0, 0)
            )
            memory_term = grad_rows[:, :mem_rows].astype(jnp.float32) + grad_rows[
                :, mem_rows + tok_rows :
            ].astype(jnp.float32)
            previous = lax.dynamic_index_in_dim(memory_out, item_slot, 0, keepdims=True)
            memory_out = lax.dynamic_update_slice(
                memory_out, jnp.where(seg_slot == 0, memory_term, previous), (item_slot, 0, 0)
            )
            return (grad_rows, grad_sums, in_store, memory_out)

        def pass_back(grad_in, grad_sums, in_store, memory_out):
            return (grad_in.astype(jnp.bfloat16), grad_sums, in_store, memory_out)

        grad_rows, grad_sums, in_store, memory_out = lax.cond(
            is_live, run_back, pass_back, grad_in, grad_sums, in_store, memory_out
        )
        grad_received = shifted(grad_rows, "section", -1)
        return (grad_store, grad_received, grad_sums, in_store, memory_out)

    cut_points = []
    bounds = [0] + cut_points + [clocks]
    carry = (
        jnp.zeros((num_items, mem_rows, D), jnp.float32),
        jnp.zeros((1, num_rows, D), jnp.bfloat16),
        blank_grads(section_params),
        jnp.zeros((num_items, segs, tok_rows, D), jnp.float32),
        jnp.zeros((num_items, mem_rows, D), jnp.float32),
    )
    shards = None
    carry = lax.fori_loop(bounds[0], bounds[1], back_tick, carry)
    grad_store, grad_received, grad_sums, in_store, memory_out = carry
    shards = lax.psum_scatter(stack_grads(grad_sums), "dp", scatter_dimension=1, tiled=True)
    first_flag = (section_id == 0).astype(jnp.float32)
    last_flag = (section_id == sections - 1).astype(jnp.float32)
    out_term = out_store * last_flag
    in_term = in_store * first_flag
    mem_term = (memory_out * first_flag)[:, None]
    out_part, in_part, mem_part = (
        lax.psum_scatter(
            out_term.astype(jnp.bfloat16), "section", scatter_dimension=3, tiled=True
        ).astype(jnp.float32),
        lax.psum_scatter(
            in_term.astype(jnp.bfloat16), "section", scatter_dimension=3, tiled=True
        ).astype(jnp.float32),
        lax.psum_scatter(
            mem_term.astype(jnp.bfloat16), "section", scatter_dimension=3, tiled=True
        ).astype(jnp.float32),
    )
    return (out_part.astype(jnp.bfloat16), in_part.astype(jnp.bfloat16), mem_part[:, 0]) + tuple(
        shards
    )


def solution(mesh):
    return jax.shard_map(
        on_device,
        mesh=mesh,
        in_specs=(
            P("dp", None, None, "section"),
            P("dp", None, None, "section"),
            P("dp", None, "section"),
            P("dp"),
            P("section", None, None),
            P("section", None, None),
            P("section", None),
            P("section", None),
            P("section", None, None),
            P("section", None),
            P("section", None, None),
            P("section", None),
            P("section", None),
        ),
        out_specs=(
            P("dp", None, None, "section"),
            P("dp", None, None, "section"),
            P("dp", None, "section"),
            P("section", "dp", None),
            P("section", "dp", None),
            P("section", "dp"),
            P("section", "dp"),
            P("section", "dp", None),
            P("section", "dp"),
            P("section", "dp", None),
            P("section", "dp"),
            P("section", "dp"),
        ),
        check_vma=False,
    )
```

profile of v0, /device:TPU:0, one launch (start us, length us, event | category | flops | bytes accessed | tf_op | source)
XLA Modules:
  0.0 2731.7 jit_solution(5534458942974426082)
XLA Ops:
  9.6 11.0 all-gather
  21.0 22.6 all-gather.4.cloned.1.call-done
  50.6 90.9 %conditional.9 = (bf16[1,522,768]{2,1,0:T(8,128)(2,1)}, f32[2,1,522,768]{3,2,1,0:T(8,128)}, bf16[2,1,522,2304]{3,2,1,0:T(8,128)(2,1)}, f32[2,1,12,522]{3,2,1,0:T...) conditional(s32[]{:T(128)} %convert_element_type.930, ...), branch_computations={%region_0.1_spmd, %region_1.8_spmd} | conditional | flops 8385856512 | bytes 193119200 | solution.py:300
  69.7 7.5 fusion
  77.1 9.1 fusion.1
  86.2 8.0 fusion.18
  115.1 16.9 fusion.636
  143.0 19.5 collective-permute-done.1
  166.4 69.3 %collective-permute-start.2 = (bf16[1,522,768]{2,1,0:T(8,128)(2,1)}, bf16[1,522,768]{2,1,0:T(8,128)(2,1)S(1)}, u32[]{:S(2)}, u32[]{:S(2)}) collective-permute-start(bf16[1,522,768]{2,1,0:T(8,128)(2,1)} %get-tuple-element.2674), channel_id=1, source_target_pairs={{0,8},{8,16},{16,24},{24,0},{1,9},{9,17},{17,25},{25,1},{2,10},{10... | collective-permute-start | bytes 2405384 | tf_op jit(solution)/shard_map/ppermute | solution.py:14
  237.9 14.9 collective-permute-done.2
  254.0 9.1 conditional.11
  267.2 15.4 collective-permute-done.3
  286.8 64.7 %collective-permute-start.4 = (bf16[1,522,768]{2,1,0:T(8,128)(2,1)}, bf16[1,522,768]{2,1,0:T(8,128)(2,1)S(1)}, u32[]{:S(2)}, u32[]{:S(2)}) collective-permute-start(bf16[1,522,768]{2,1,0:T(8,128)(2,1)} %get-tuple-element.2692), channel_id=1, source_target_pairs={{0,8},{8,16},{16,24},{24,0},{1,9},{9,17},{17,25},{25,1},{2,10},{10... | collective-permute-start | bytes 2405384 | tf_op jit(solution)/shard_map/ppermute | solution.py:14
  354.3 84.1 %collective-permute-done.4 = bf16[1,522,768]{2,1,0:T(8,128)(2,1)S(1)} collective-permute-done((bf16[1,522,768]{2,1,0:T(8,128)(2,1)}, bf16[1,522,768]{2,1,0:T(8,128)(2,1)S(1)}, u32[]{:S(2)}, u32[]{:S(2)}) %collective-permute-start.4) | collective-permute-done | bytes 801824 | tf_op jit(solution)/shard_map/ppermute | solution.py:14
  440.1 73.3 %conditional.13 = ((bf16[1,522,768]{2,1,0:T(8,128)(2,1)}, f32[2,1,522,768]{3,2,1,0:T(8,128)}, bf16[2,1,522,2304]{3,2,1,0:T(8,128)(2,1)}, f32[2,1,12,522]{3,2,1,0...) conditional(s32[]{:T(128)} %convert_element_type.936, ...), branch_computations={%region_32.33_spmd, %region_33.40_spmd} | conditional | flops 8385856512 | bytes 146964512 | solution.py:300
  453.0 7.5 fusion.244
  460.5 9.1 fusion.245
  469.6 8.0 fusion.262
  488.8 16.8 fusion.644
  516.1 20.0 collective-permute-done.5
  537.3 9.1 conditional.14
  546.4 63.6 %collective-permute-start.6 = (bf16[1,522,768]{2,1,0:T(8,128)(2,1)}, bf16[1,522,768]{2,1,0:T(8,128)(2,1)S(1)}, u32[]{:S(2)}, u32[]{:S(2)}) collective-permute-start(bf16[1,522,768]{2,1,0:T(8,128)(2,1)} %get-tuple-element.2710), channel_id=1, source_target_pairs={{0,8},{8,16},{16,24},{24,0},{1,9},{9,17},{17,25},{25,1},{2,10},{10... | collective-permute-start | bytes 2405384 | tf_op jit(solution)/shard_map/ppermute | solution.py:14
  611.4 10.0 collective-permute-done.6
  639.3 13.6 conditional.16
  642.0 8.3 copy.264
  676.2 1476.1 %while.41 = (s32[]{:T(128)}, f32[1,10,768]{2,1,0:T(8,128)}, bf16[1,522,768]{2,1,0:T(8,128)(2,1)S(1)}, f32[768,2304]{1,0:T(8,128)}, f32[768,768]{1,0:T(8,128)}, /...) while((s32[]{:T(128)}, f32[1,10,768]{2,1,0:T(8,128)}, ...), condition=%wide.region_82.83_spmd.clone, body=%wide.region_65.82_spmd.clone.sunk | while | flops 17160814592 | bytes 505884160 | solution.py:382
  684.2 291.0 %collective-permute-start = (bf16[1,522,768]{2,1,0:T(8,128)(2,1)S(1)}, bf16[1,522,768]{2,1,0:T(8,128)(2,1)S(1)}, u32[]{:S(2)}, u32[]{:S(2)}) collective-permute-start(bf16[1,522,768]{2,1,0:T(8,128)(2,1)S(1)} %convert_element_type.1209), channel_id=1, source_target_pairs={{0,24},{8,0},{16,8},{24,16},{1,25},{9,1},{17,9},{25,17},{2,26},{10... | collective-permute-start | bytes 2405384 | tf_op jit(solution)/shard_map/while/body/eval_jaxpr/ppermute | solution.py:14
  975.2 9.8 collective-permute-done
  996.2 9.8 collective-permute-done
  1011.0 144.1 %collective-permute-start = (bf16[1,522,768]{2,1,0:T(8,128)(2,1)S(1)}, bf16[1,522,768]{2,1,0:T(8,128)(2,1)S(1)}, u32[]{:S(2)}, u32[]{:S(2)}) collective-permute-start(bf16[1,522,768]{2,1,0:T(8,128)(2,1)S(1)} %convert_element_type.1209), channel_id=1, source_target_pairs={{0,24},{8,0},{16,8},{24,16},{1,25},{9,1},{17,9},{25,17},{2,26},{10... | collective-permute-start | bytes 2405384 | tf_op jit(solution)/shard_map/while/body/eval_jaxpr/ppermute | solution.py:14
  1155.0 158.6 %collective-permute-done = bf16[1,522,768]{2,1,0:T(8,128)(2,1)S(1)} collective-permute-done((bf16[1,522,768]{2,1,0:T(8,128)(2,1)S(1)}, bf16[1,522,768]{2,1,0:T(8,128)(2,1)S(1)}, u32[]{:S(2)}, u32[]{:S(2)}) %collective-permute-start) | collective-permute-done | bytes 801824 | tf_op jit(solution)/shard_map/while/body/eval_jaxpr/ppermute | solution.py:14
  1318.1 148.1 %conditional.19 = ((f32[768,2304]{1,0:T(8,128)}, f32[768,768]{1,0:T(8,128)}, f32[768]{0:T(1024)}, f32[768]{0:T(1024)}, f32[768,3072]{1,0:T(8,128)}, /*index=5*/f...) conditional(s32[]{:T(128)} %convert_element_type.1208, ...), branch_computations={%region_66.66_spmd, %region_67.81_spmd} | conditional | flops 17157988352 | bytes 493788992 | solution.py:366
  1339.7 19.8 convert_reduce_fusion
  1359.6 21.6 convolution_add_fusion.1
  1396.7 13.3 convolution_add_fusion.2
  1410.0 9.1 fusion.562
  1419.2 12.1 multiply_reduce_fusion.16
  1431.3 9.8 multiply_convert_fusion
  1466.4 12.8 collective-permute-done
  1487.4 144.8 %collective-permute-start = (bf16[1,522,768]{2,1,0:T(8,128)(2,1)S(1)}, bf16[1,522,768]{2,1,0:T(8,128)(2,1)S(1)}, u32[]{:S(2)}, u32[]{:S(2)}) collective-permute-start(bf16[1,522,768]{2,1,0:T(8,128)(2,1)S(1)} %convert_element_type.1209), channel_id=1, source_target_pairs={{0,24},{8,0},{16,8},{24,16},{1,25},{9,1},{17,9},{25,17},{2,26},{10... | collective-permute-start | bytes 2405384 | tf_op jit(solution)/shard_map/while/body/eval_jaxpr/ppermute | solution.py:14
  1632.2 11.5 collective-permute-done
  1654.1 9.8 collective-permute-done
  1668.7 156.8 %collective-permute-start = (bf16[1,522,768]{2,1,0:T(8,128)(2,1)S(1)}, bf16[1,522,768]{2,1,0:T(8,128)(2,1)S(1)}, u32[]{:S(2)}, u32[]{:S(2)}) collective-permute-start(bf16[1,522,768]{2,1,0:T(8,128)(2,1)S(1)} %convert_element_type.1209), channel_id=1, source_target_pairs={{0,24},{8,0},{16,8},{24,16},{1,25},{9,1},{17,9},{25,17},{2,26},{10... | collective-permute-start | bytes 2405384 | tf_op jit(solution)/shard_map/while/body/eval_jaxpr/ppermute | solution.py:14
  1825.5 156.1 %collective-permute-done = bf16[1,522,768]{2,1,0:T(8,128)(2,1)S(1)} collective-permute-done((bf16[1,522,768]{2,1,0:T(8,128)(2,1)S(1)}, bf16[1,522,768]{2,1,0:T(8,128)(2,1)S(1)}, u32[]{:S(2)}, u32[]{:S(2)}) %collective-permute-start) | collective-permute-done | bytes 801824 | tf_op jit(solution)/shard_map/while/body/eval_jaxpr/ppermute | solution.py:14
  1986.1 147.9 %conditional.19 = ((f32[768,2304]{1,0:T(8,128)}, f32[768,768]{1,0:T(8,128)}, f32[768]{0:T(1024)}, f32[768]{0:T(1024)}, f32[768,3072]{1,0:T(8,128)}, /*index=5*/f...) conditional(s32[]{:T(128)} %convert_element_type.1208, ...), branch_computations={%region_66.66_spmd, %region_67.81_spmd} | conditional | flops 17157988352 | bytes 493788992 | solution.py:366
  2007.7 19.9 convert_reduce_fusion
  2027.7 21.4 convolution_add_fusion.1
  2064.6 13.3 convolution_add_fusion.2
  2077.9 9.1 fusion.562
  2087.0 12.1 multiply_reduce_fusion.16
  2099.1 9.8 multiply_convert_fusion
  2126.7 7.1 convolution_add_fusion
  2134.2 12.2 collective-permute-done
  2184.9 30.2 %reduce-scatter.43.cloned.1.call-done = f32[96,1]{1,0:T(8,128)} async-done(((f32[768,1]{1,0:T(8,128)}), f32[96,1]{1,0:T(8,128)}) %reduce-scatter.43.cloned.1.call-update) | async-done | bytes 400
  2216.5 30.2 %reduce-scatter.45.cloned.1.call-done = f32[96,1]{1,0:T(8,128)} async-done(((f32[768,1]{1,0:T(8,128)}), f32[96,1]{1,0:T(8,128)}) %reduce-scatter.45.cloned.1.call-update) | async-done | bytes 400
  2248.1 29.7 %reduce-scatter.49.cloned.1.call-done = f32[96,1]{1,0:T(8,128)} async-done(((f32[768,1]{1,0:T(8,128)}), f32[96,1]{1,0:T(8,128)}) %reduce-scatter.49.cloned.1.call-update) | async-done | bytes 400
  2279.2 33.3 %reduce-scatter.47.cloned.1.call-done = f32[384,1]{1,0:T(8,128)} async-done(((f32[3072,1]{1,0:T(8,128)}), f32[384,1]{1,0:T(8,128)}) %reduce-scatter.47.cloned.1.call-update) | async-done | bytes 1552
  2314.1 23.2 reduce-scatter.41.cloned.1.call-done
  2339.7 31.5 %reduce-scatter.37.cloned.1.call-done = bf16[192,1004]{1,0:T(8,128)(2,1)} async-done(((bf16[768,1004]{1,0:T(8,128)(2,1)}), bf16[192,1004]{1,0:T(8,128)(2,1)}) %reduce-scatter.37.cloned.1.call-update) | async-done | bytes 385552
  2373.4 31.6 %reduce-scatter.39.cloned.1.call-done = bf16[192,1004]{1,0:T(8,128)(2,1)} async-done(((bf16[768,1004]{1,0:T(8,128)(2,1)}), bf16[192,1004]{1,0:T(8,128)(2,1)}) %reduce-scatter.39.cloned.1.call-update) | async-done | bytes 385552
  2407.1 37.0 %reduce-scatter.31.cloned.1.call-done = f32[1,96,768]{2,1,0:T(8,128)} async-done(((f32[1,768,768]{2,1,0:T(8,128)}), f32[1,96,768]{2,1,0:T(8,128)}) %reduce-scatter.31.cloned.1.call-update) | async-done | bytes 294928 | tf_op jit(solution)/shard_map/reduce_scatter | solution.py:384
  2444.2 79.3 %reduce-scatter.29.cloned.1.call-done = f32[1,96,2304]{2,1,0:T(8,128)} async-done(((f32[1,768,2304]{2,1,0:T(8,128)}), f32[1,96,2304]{2,1,0:T(8,128)}) %reduce-scatter.29.cloned.1.call-update) | async-done | bytes 884752 | tf_op jit(solution)/shard_map/reduce_scatter | solution.py:384
  2523.4 100.8 %reduce-scatter.33.cloned.1.call-done = f32[1,96,3072]{2,1,0:T(8,128)} async-done(((f32[1,768,3072]{2,1,0:T(8,128)}), f32[1,96,3072]{2,1,0:T(8,128)}) %reduce-scatter.33.cloned.1.call-update) | async-done | bytes 1179664 | tf_op jit(solution)/shard_map/reduce_scatter | solution.py:384
  2624.2 100.6 %reduce-scatter.35.cloned.1.call-done = f32[1,384,768]{2,1,0:T(8,128)} async-done(((f32[1,3072,768]{2,1,0:T(8,128)}), f32[1,384,768]{2,1,0:T(8,128)}) %reduce-scatter.35.cloned.1.call-update) | async-done | bytes 1179664 | tf_op jit(solution)/shard_map/reduce_scatter | solution.py:384
  (521 shorter events, 375.8 us)
Async XLA Ops:
  7.2 36.4 %all-gather.4.cloned.1.call-start = ((), (), s32[]{:S(2)}) async-start(), calls=%async_computation.12 | async-start | bytes 1966080 | tf_op jit(solution)/shard_map/all_gather | solution.py:253
  7.9 620.3 %all-gather.6.cloned.1.call-start = ((), (), s32[]{:S(2)}) async-start(), calls=%async_computation.13 | async-start | bytes 1966080 | tf_op jit(solution)/shard_map/all_gather | solution.py:254
  20.9 28.6 %copy-start.45 = (pred[1,10]{1,0:T(4,128)(4,1)}, pred[1,10]{1,0:T(4,128)(4,1)S(1)}, u32[]{:S(2)}) copy-start(pred[1,10]{1,0:T(4,128)(4,1)S(1)} %broadcast.3341) | copy-start | bytes 34
  21.0 29.6 %copy-start.38 = (f32[1,768]{1,0:T(1,128)S(1)}, f32[1,768]{1,0:T(1,128)}, u32[]{:S(2)}) copy-start(f32[1,768]{1,0:T(1,128)} %param.45) | copy-start | bytes 9220
  21.0 29.6 %copy-start.50 = (f32[1,3072]{1,0:T(1,128)S(1)}, f32[1,3072]{1,0:T(1,128)}, u32[]{:S(2)}) copy-start(f32[1,3072]{1,0:T(1,128)} %param.42) | copy-start | bytes 36868
  86.2 11.7 copy-start.17
  103.6 11.5 slice-start.17
  141.5 21.0 collective-permute-start.1
  163.7 72.1 %copy-start.46 = (pred[1,10]{1,0:T(4,128)(4,1)S(1)}, pred[1,10]{1,0:T(4,128)(4,1)}, u32[]{:S(2)}) copy-start(pred[1,10]{1,0:T(4,128)(4,1)} %copy-done.45) | copy-start | bytes 34
  166.4 86.4 %collective-permute-start.2 = (bf16[1,522,768]{2,1,0:T(8,128)(2,1)}, bf16[1,522,768]{2,1,0:T(8,128)(2,1)S(1)}, u32[]{:S(2)}, u32[]{:S(2)}) collective-permute-start(bf16[1,522,768]{2,1,0:T(8,128)(2,1)} %get-tuple-element.2674), channel_id=1, source_target_pairs={{0,8},{8,16},{16,24},{24,0},{1,9},{9,17},{17,25},{25,1},{2,10},{10... | collective-permute-start | bytes 2405384 | tf_op jit(solution)/shard_map/ppermute | solution.py:14
  263.1 19.5 collective-permute-start.3
  286.8 153.3 %copy-start.44 = (pred[1,522]{1,0:T(4,128)(4,1)S(1)}, pred[1,522]{1,0:T(4,128)(4,1)}, u32[]{:S(2)}) copy-start(pred[1,522]{1,0:T(4,128)(4,1)} %get-tuple-element.3245) | copy-start | bytes 1570
  286.8 151.6 %collective-permute-start.4 = (bf16[1,522,768]{2,1,0:T(8,128)(2,1)}, bf16[1,522,768]{2,1,0:T(8,128)(2,1)S(1)}, u32[]{:S(2)}, u32[]{:S(2)}) collective-permute-start(bf16[1,522,768]{2,1,0:T(8,128)(2,1)} %get-tuple-element.2692), channel_id=1, source_target_pairs={{0,8},{8,16},{16,24},{24,0},{1,9},{9,17},{17,25},{25,1},{2,10},{10... | collective-permute-start | bytes 2405384 | tf_op jit(solution)/shard_map/ppermute | solution.py:14
  440.1 73.3 %copy-start.33 = (bf16[1,2,502,192]{2,3,1,0:T(8,128)(2,1)S(1)}, bf16[1,2,502,192]{2,3,1,0:T(8,128)(2,1)}, u32[]{:S(2)}) copy-start(bf16[1,2,502,192]{2,3,1,0:T(8,128)(2,1)} %param.34) | copy-start | bytes 1156612
  440.1 97.2 %copy-start.43 = (pred[1,522]{1,0:T(4,128)(4,1)S(1)}, pred[1,522]{1,0:T(4,128)(4,1)}, u32[]{:S(2)}) copy-start(pred[1,522]{1,0:T(4,128)(4,1)} %get-tuple-element.3246) | copy-start | bytes 1570
  513.4 22.7 collective-permute-start.5
  514.6 1668.9 %reduce-scatter.51.cloned.1.call-start = ((), (), s32[]{:S(2)}) async-start(), calls=%async_computation.25 | async-start | bytes 442368
  537.3 85.4 %copy-start.42 = (pred[1,522]{1,0:T(4,128)(4,1)S(1)}, pred[1,522]{1,0:T(4,128)(4,1)}, u32[]{:S(2)}) copy-start(pred[1,522]{1,0:T(4,128)(4,1)} %get-tuple-element.3247) | copy-start | bytes 1570
  546.4 75.0 %collective-permute-start.6 = (bf16[1,522,768]{2,1,0:T(8,128)(2,1)}, bf16[1,522,768]{2,1,0:T(8,128)(2,1)S(1)}, u32[]{:S(2)}, u32[]{:S(2)}) collective-permute-start(bf16[1,522,768]{2,1,0:T(8,128)(2,1)} %get-tuple-element.2710), channel_id=1, source_target_pairs={{0,8},{8,16},{16,24},{24,0},{1,9},{9,17},{17,25},{25,1},{2,10},{10... | collective-permute-start | bytes 2405384 | tf_op jit(solution)/shard_map/ppermute | solution.py:14
  622.6 16.6 copy-start.41
  625.7 13.4 collective-permute-start.7
  652.9 14.2 copy-start.10
  684.2 300.8 %collective-permute-start = (bf16[1,522,768]{2,1,0:T(8,128)(2,1)S(1)}, bf16[1,522,768]{2,1,0:T(8,128)(2,1)S(1)}, u32[]{:S(2)}, u32[]{:S(2)}) collective-permute-start(bf16[1,522,768]{2,1,0:T(8,128)(2,1)S(1)} %convert_element_type.1209), channel_id=1, source_target_pairs={{0,24},{8,0},{16,8},{24,16},{1,25},{9,1},{17,9},{25,17},{2,26},{10... | collective-permute-start | bytes 2405384 | tf_op jit(solution)/shard_map/while/body/eval_jaxpr/ppermute | solution.py:14
  989.9 16.1 collective-permute-start
  1011.0 302.6 %collective-permute-start = (bf16[1,522,768]{2,1,0:T(8,128)(2,1)S(1)}, bf16[1,522,768]{2,1,0:T(8,128)(2,1)S(1)}, u32[]{:S(2)}, u32[]{:S(2)}) collective-permute-start(bf16[1,522,768]{2,1,0:T(8,128)(2,1)S(1)} %convert_element_type.1209), channel_id=1, source_target_pairs={{0,24},{8,0},{16,8},{24,16},{1,25},{9,1},{17,9},{25,17},{2,26},{10... | collective-permute-start | bytes 2405384 | tf_op jit(solution)/shard_map/while/body/eval_jaxpr/ppermute | solution.py:14
  1328.1 11.5 slice-start.31
  1335.5 24.0 slice-start
  1339.7 19.9 slice-start.1
  1339.7 19.9 slice-start.2
  1359.6 25.4 copy-start.51
  1359.6 25.4 copy-start.29
  1359.6 25.4 copy-start.28
  1359.6 25.4 copy-start.31
  1359.6 25.4 copy-start.32
  1359.6 25.4 copy-start.47
  1396.7 13.3 copy-start.1
  1431.3 9.9 copy-start.2
  1466.3 12.9 collective-permute-start
  1487.4 156.3 %collective-permute-start = (bf16[1,522,768]{2,1,0:T(8,128)(2,1)S(1)}, bf16[1,522,768]{2,1,0:T(8,128)(2,1)S(1)}, u32[]{:S(2)}, u32[]{:S(2)}) collective-permute-start(bf16[1,522,768]{2,1,0:T(8,128)(2,1)S(1)} %convert_element_type.1209), channel_id=1, source_target_pairs={{0,24},{8,0},{16,8},{24,16},{1,25},{9,1},{17,9},{25,17},{2,26},{10... | collective-permute-start | bytes 2405384 | tf_op jit(solution)/shard_map/while/body/eval_jaxpr/ppermute | solution.py:14
  1648.8 15.1 collective-permute-start
  1668.7 312.9 %collective-permute-start = (bf16[1,522,768]{2,1,0:T(8,128)(2,1)S(1)}, bf16[1,522,768]{2,1,0:T(8,128)(2,1)S(1)}, u32[]{:S(2)}, u32[]{:S(2)}) collective-permute-start(bf16[1,522,768]{2,1,0:T(8,128)(2,1)S(1)} %convert_element_type.1209), channel_id=1, source_target_pairs={{0,24},{8,0},{16,8},{24,16},{1,25},{9,1},{17,9},{25,17},{2,26},{10... | collective-permute-start | bytes 2405384 | tf_op jit(solution)/shard_map/while/body/eval_jaxpr/ppermute | solution.py:14
  1996.1 11.5 slice-start.31
  2003.6 24.0 slice-start
  2007.7 19.9 slice-start.1
  2007.7 19.9 slice-start.2
  2027.6 25.2 copy-start.51
  2027.6 25.2 copy-start.29
  2027.6 25.2 copy-start.28
  2027.6 25.2 copy-start.31
  2027.6 25.2 copy-start.32
  2027.6 25.2 copy-start.47
  2064.5 13.3 copy-start.1
  2134.1 12.3 collective-permute-start
  2153.9 61.2 %reduce-scatter.43.cloned.1.call-start = ((), (), s32[]{:S(2)}) async-start(), calls=%async_computation.21 | async-start | bytes 442368
  2155.6 91.1 %reduce-scatter.45.cloned.1.call-start = ((), (), s32[]{:S(2)}) async-start(), calls=%async_computation.22 | async-start | bytes 442368
  2157.3 120.5 %reduce-scatter.49.cloned.1.call-start = ((), (), s32[]{:S(2)}) async-start(), calls=%async_computation.24 | async-start | bytes 442368
  2158.9 153.6 %reduce-scatter.47.cloned.1.call-start = ((), (), s32[]{:S(2)}) async-start(), calls=%async_computation.23 | async-start | bytes 1769472
  2165.3 172.0 %reduce-scatter.41.cloned.1.call-start = ((), (), s32[]{:S(2)}) async-start(), calls=%async_computation.20 | async-start | bytes 245760
  2167.8 203.4 %reduce-scatter.37.cloned.1.call-start = ((), (), s32[]{:S(2)}) async-start(), calls=%async_computation.18 | async-start | bytes 1966080
  2174.2 230.8 %reduce-scatter.39.cloned.1.call-start = ((), (), s32[]{:S(2)}) async-start(), calls=%async_computation.19 | async-start | bytes 1966080
  2180.5 263.7 %reduce-scatter.31.cloned.1.call-start = ((), (), s32[]{:S(2)}) async-start(), calls=%async_computation.15 | async-start | bytes 2654208 | tf_op jit(solution)/shard_map/reduce_scatter | solution.py:384
  2181.2 342.2 %reduce-scatter.29.cloned.1.call-start = ((), (), s32[]{:S(2)}) async-start(), calls=%async_computation.14 | async-start | bytes 7962624 | tf_op jit(solution)/shard_map/reduce_scatter | solution.py:384
  2181.8 442.4 %reduce-scatter.33.cloned.1.call-start = ((), (), s32[]{:S(2)}) async-start(), calls=%async_computation.16 | async-start | bytes 10616832 | tf_op jit(solution)/shard_map/reduce_scatter | solution.py:384
  2182.6 542.3 %reduce-scatter.35.cloned.1.call-start = ((), (), s32[]{:S(2)}) async-start(), calls=%async_computation.17 | async-start | bytes 10616832 | tf_op jit(solution)/shard_map/reduce_scatter | solution.py:384
  (60 other events, 326.6 us)
Sparse Core Ops, SparseCore 0:
  9.9 33.6 all-gather.3
  514.7 38.5 all-gather.5
  2154.0 29.4 reduce-scatter.50
  2186.3 28.8 reduce-scatter.42
  2217.8 28.8 reduce-scatter.44
  2248.9 28.8 reduce-scatter.48
  2280.1 32.3 reduce-scatter.46
  2315.3 21.9 reduce-scatter.40
  2340.3 30.8 reduce-scatter.36
  2374.0 30.8 reduce-scatter.38
  2407.9 36.2 reduce-scatter.30
  2446.9 76.4 reduce-scatter.28
  2526.3 97.8 reduce-scatter.32
  2626.9 97.8 reduce-scatter.34
where the time goes:
time: 2730 us
  waiting for transfers between devices  1100 us (40%)
  starting transfers between devices  952 us (35%)
  matrix products  304 us (11%)
  other arithmetic  156 us (6%)
  local copies, waits for them, and re-layouts  142 us (5%)
  loops' own time  47.8 us (2%)
    ppermute x15, starting transfers between devices, shifted(): lax.ppermute(value, axis, [(i, (i + by) % devices) for i in range(devices)])  951 us
    ppermute x15, waiting for transfers between devices, shifted(): lax.ppermute(value, axis, [(i, (i + by) % devices) for i in range(devices)])  550 us
    reduce_scatter x4, waiting for transfers between devices, on_device(): lax.psum_scatter(stack_grads(grad_sums), 'dp', scatter_dimension=1, tiled...  318 us
    unnamed x22, waiting for transfers between devices  213 us
  transfers between devices with their start and end apart: 29, of which 28 were waited for; matrix products, arithmetic and copies ran while one was open for 2% of the time, Pallas kernels for 0%

commit v1 on v0

v1 whole, which is shorter than its diff:
```python
import functools

import jax
import jax.numpy as jnp
from jax import lax
from jax.experimental import pallas as pl
from jax.experimental.pallas import tpu as pltpu
from jax.sharding import PartitionSpec as P

D = 768
H = 12
HEAD = 64
FF = 3072
PAIRS = H // 2
WIDE = 2 * HEAD
STEP = 256
BLOCK = 16
BF = jnp.bfloat16
F32 = jnp.float32
MESH = pl.DeviceIdType.MESH
ANY = pl.BlockSpec(memory_space=pl.ANY)
VMEM = pl.BlockSpec(memory_space=pltpu.VMEM)
VMEM_LIMIT = 63 * 1024 * 1024


def dot(a, b):
    return jnp.dot(a, b, preferred_element_type=F32)


def dot_nt(a, b):
    return lax.dot_general(a, b, (((1,), (1,)), ((), ())), preferred_element_type=F32)


def dot_tn(a, b):
    return lax.dot_general(a, b, (((0,), (0,)), ((), ())), preferred_element_type=F32)


def cols(index):
    return pl.ds(index * STEP, STEP)


def remote(src, dst, send, recv, target):
    return pltpu.make_async_remote_copy(
        src_ref=src, dst_ref=dst, send_sem=send, recv_sem=recv, device_id=target, device_id_type=MESH
    )


class Place:
    def __init__(self, sections):
        self.s = lax.axis_index("section")
        self.d = lax.axis_index("dp")
        self.c = lax.rem(self.d, 2)
        self.base = self.d - self.c
        self.other = self.base + 1 - self.c
        self.next = lax.rem(self.s + 1, sections)
        self.prev = lax.rem(self.s + sections - 1, sections)


def plane_barrier(place, sections):
    barrier = pltpu.get_barrier_semaphore()
    for section in range(sections):
        for core in range(2):

            @pl.when((place.s != section) | (place.c != core))
            def _():
                pl.semaphore_signal(
                    barrier, inc=1, device_id=(section, place.base + core), device_id_type=MESH
                )

    pl.semaphore_wait(barrier, 2 * sections - 1)


def spread_kernel(sections, a_ref, g_ref, len_ref, x_ref, gr_ref, lens_ref, send, got_x, got_g, got_l, local):
    place = Place(sections)
    s, c = place.s, place.c
    plane_barrier(place, sections)
    moves = []
    for core in range(2):
        for which, (src, dst, target, got) in enumerate(
            ((a_ref, x_ref, 0, got_x), (g_ref, gr_ref, sections - 1, got_g))
        ):
            here = (s == target) & (c == core)
            slot = 2 * which + core
            far = remote(
                src.at[core], dst.at[c, s], send.at[slot], got.at[c, s], (target, place.base + core)
            )
            near = pltpu.make_async_copy(src.at[core], dst.at[c, s], local.at[which])
            moves.append((here, far, near))
    for here, far, near in moves:
        pl.when(jnp.logical_not(here))(far.start)
        pl.when(here)(near.start)
    far_len = remote(len_ref, lens_ref.at[c], send.at[4], got_l.at[0], (s, place.other))
    near_len = pltpu.make_async_copy(len_ref, lens_ref.at[c], local.at[2])
    far_len.start()
    near_len.start()
    for here, far, near in moves:
        pl.when(jnp.logical_not(here))(far.wait_send)
        pl.when(here)(near.wait)
    for which, (src, dst, target, got) in enumerate(
        ((a_ref, x_ref, 0, got_x), (g_ref, gr_ref, sections - 1, got_g))
    ):
        for core in range(2):
            for section in range(sections):

                @pl.when((s == target) & ((c != core) | (s != section)))
                def _():
                    remote(
                        src.at[0], dst.at[core, section], send.at[0], got.at[core, section], (s, place.d)
                    ).wait_recv()

    far_len.wait_send()
    near_len.wait()
    remote(len_ref, lens_ref.at[1 - c], send.at[4], got_l.at[0], (s, place.other)).wait_recv()


def spread(sections, a, g, length_tile):
    half = a.shape[2]
    block = (2, sections) + a.shape[1:]
    return pl.pallas_call(
        functools.partial(spread_kernel, sections),
        name="spread_items",
        out_shape=(
            jax.ShapeDtypeStruct(block, BF),
            jax.ShapeDtypeStruct(block, BF),
            jax.ShapeDtypeStruct((2, 8, 128), F32),
        ),
        in_specs=[ANY, ANY, ANY],
        out_specs=(ANY, ANY, ANY),
        scratch_shapes=[
            pltpu.SemaphoreType.DMA((5,)),
            pltpu.SemaphoreType.DMA((2, sections)),
            pltpu.SemaphoreType.DMA((2, sections)),
            pltpu.SemaphoreType.DMA((1,)),
            pltpu.SemaphoreType.DMA((3,)),
        ],
        compiler_params=pltpu.CompilerParams(collective_id=0, has_side_effects=True),
    )(a, g, length_tile)


def collect_kernel(sections, h_ref, x_ref, m_ref, oh_ref, ox_ref, om_ref, send, got_h, got_x, got_m, local):
    place = Place(sections)
    s, c = place.s, place.c
    plane_barrier(place, sections)
    last = sections - 1
    jobs = (
        (h_ref, oh_ref, last, got_h, 0),
        (x_ref, ox_ref, 0, got_x, 1),
    )
    for src, dst, origin, got, which in jobs:
        for item in range(2):
            for section in range(sections):
                here = (s == section) & (c == item)
                mine = s == origin
                far = remote(
                    src.at[item, section], dst.at[c], send.at[which, item, section], got.at[c], (section, place.base + item)
                )
                near = pltpu.make_async_copy(src.at[item, section], dst.at[c], local.at[which])
                pl.when(mine & jnp.logical_not(here))(far.start)
                pl.when(mine & here)(near.start)
    for item in range(2):
        for section in range(sections):
            here = (s == section) & (c == item)
            mine = (s == 0) & (c == 0)
            far = remote(
                m_ref.at[item, section], om_ref, send.at[2, item, section], got_m.at[0], (section, place.base + item)
            )
            near = pltpu.make_async_copy(m_ref.at[item, section], om_ref, local.at[2])
            pl.when(mine & jnp.logical_not(here))(far.start)
            pl.when(mine & here)(near.start)
    for src, dst, origin, got, which in jobs:
        for item in range(2):
            for section in range(sections):
                here = (s == section) & (c == item)
                mine = s == origin
                far = remote(
                    src.at[item, section], dst.at[c], send.at[which, item, section], got.at[c], (section, place.base + item)
                )
                near = pltpu.make_async_copy(src.at[item, section], dst.at[c], local.at[which])
                pl.when(mine & jnp.logical_not(here))(far.wait_send)
                pl.when(mine & here)(near.wait)
        for core in range(2):

            @pl.when((s != origin) | (c != core))
            def _():
                remote(
                    src.at[0, 0], dst.at[core], send.at[which, 0, 0], got.at[core], (s, place.d)
                ).wait_recv()

    for item in range(2):
        for section in range(sections):
            here = (s == section) & (c == item)
            mine = (s == 0) & (c == 0)
            far = remote(
                m_ref.at[item, section], om_ref, send.at[2, item, section], got_m.at[0], (section, place.base + item)
            )
            near = pltpu.make_async_copy(m_ref.at[item, section], om_ref, local.at[2])
            pl.when(mine & jnp.logical_not(here))(far.wait_send)
            pl.when(mine & here)(near.wait)

    @pl.when((s != 0) | (c != 0))
    def _():
        remote(m_ref.at[0, 0], om_ref, send.at[2, 0, 0], got_m.at[0], (s, place.d)).wait_recv()


def collect(sections, h, x, m):
    block = (2,) + h.shape[2:]
    return pl.pallas_call(
        functools.partial(collect_kernel, sections),
        name="collect_results",
        out_shape=(
            jax.ShapeDtypeStruct(block, BF),
            jax.ShapeDtypeStruct(block, BF),
            jax.ShapeDtypeStruct(m.shape[2:], F32),
        ),
        in_specs=[ANY, ANY, ANY],
        out_specs=(ANY, ANY, ANY),
        scratch_shapes=[
            pltpu.SemaphoreType.DMA((3, 2, sections)),
            pltpu.SemaphoreType.DMA((2,)),
            pltpu.SemaphoreType.DMA((2,)),
            pltpu.SemaphoreType.DMA((1,)),
            pltpu.SemaphoreType.DMA((3,)),
        ],
        compiler_params=pltpu.CompilerParams(collective_id=1, has_side_effects=True),
    )(h, x, m)


def key_bias(geometry, segment, length):
    mem, slot, tok, rows = geometry
    row = lax.broadcasted_iota(jnp.int32, (1, rows), 1)
    position = row - 2 * slot + segment * tok
    is_token = (row >= 2 * slot) & (row < 2 * slot + tok) & (position.astype(F32) < length)
    is_memory = (row < mem) | ((row >= slot) & (row < slot + mem))
    return jnp.where(is_token | is_memory, 0.0, -1e30)


def stacked_pair(pair):
    lane = lax.broadcasted_iota(jnp.int32, pair.shape, 1)
    zero = jnp.zeros_like(pair)
    return jnp.concatenate(
        [jnp.where(lane < HEAD, pair, zero), jnp.where(lane >= HEAD, pair, zero)], axis=0
    )


def folded_pair(both):
    half = both.shape[0] // 2
    lane = lax.broadcasted_iota(jnp.int32, (half, WIDE), 1)
    return jnp.where(lane < HEAD, both[:half], both[half:])


def pair_probs(queries, keys, bias, s_ref, p_ref, base=()):
    s_ref[...] = dot_nt(stacked_pair(queries * jnp.asarray(HEAD**-0.5, BF)), keys)
    total = s_ref.shape[0]
    for start in range(0, total, 2 * BLOCK):
        span = pl.ds(start, 2 * BLOCK)
        scores = s_ref[span, :] + bias
        exponent = jnp.exp(scores - jnp.max(scores, axis=-1, keepdims=True))
        inverse = 1.0 / jnp.sum(exponent, axis=-1, keepdims=True)
        p_ref[base + (span, slice(None))] = (exponent * inverse).astype(BF)


def normalized(rows):
    center = rows - jnp.mean(rows, axis=-1, keepdims=True)
    spread_of = jnp.mean(center * center, axis=-1, keepdims=True)
    scale = lax.rsqrt(spread_of + 1e-06)
    return center * scale, scale


def row_blocks(half):
    return [pl.ds(start, BLOCK) for start in range(0, half, BLOCK)]


def forward_kernel(
    segment,
    sections,
    geometry,
    x0_ref,
    memory_ref,
    lens_ref,
    w_qkv,
    w_proj,
    w_in,
    w_down,
    gain_one,
    shift_one,
    b_in,
    gain_two,
    shift_two,
    o_x,
    o_q,
    o_kv,
    o_att,
    o_nb,
    o_act,
    o_gp,
    o_s1,
    o_s2,
    o_hid,
    o_mem,
    vqkv,
    vproj,
    vin,
    vdown,
    xb,
    qb,
    kvb,
    attb,
    nbb,
    actb,
    gpb,
    preb,
    s1b,
    s2b,
    hb,
    nf,
    memb,
    s_tmp,
    p_tmp,
    wsem,
    xsem,
    osem,
    kv_send,
    kv_recv,
    h_send,
    h_recv,
    m_send,
    m_recv,
):
    place = Place(sections)
    s, c = place.s, place.c
    mem, slot, tok, rows = geometry
    half = rows // 2
    own = pl.ds(pl.multiple_of(c * half, BLOCK), half)
    last = sections - 1
    weights = [
        pltpu.make_async_copy(src, dst, wsem.at[k])
        for k, (src, dst) in enumerate(((w_qkv, vqkv), (w_proj, vproj), (w_in, vin), (w_down, vdown)))
    ]

    @pl.when(s == 0)
    def _():
        for item in range(2):
            pltpu.make_async_copy(x0_ref.at[item], xb.at[item], xsem.at[item]).start()

    for copy in weights:
        copy.start()
    barrier = pltpu.get_barrier_semaphore()
    pl.semaphore_signal(barrier, inc=1, device_id=(place.prev, place.d), device_id_type=MESH)
    pl.semaphore_signal(barrier, inc=1, device_id=(s, place.other), device_id_type=MESH)
    pl.semaphore_wait(barrier, 2)

    def outgoing(item):
        pairs = (
            (xb, o_x),
            (qb, o_q),
            (kvb, o_kv),
            (attb, o_att),
            (nbb, o_nb),
            (actb, o_act),
            (gpb, o_gp),
            (s1b, o_s1),
            (s2b, o_s2),
            (hb, o_hid),
        )
        return [
            pltpu.make_async_copy(src.at[item], dst.at[item], osem.at[item, k])
            for k, (src, dst) in enumerate(pairs)
        ]

    def handoff(item):
        return remote(hb.at[item], xb.at[item], h_send.at[item], h_recv.at[item], (place.next, place.d))

    def memory_move(item):
        return remote(
            hb.at[item, pl.ds(slot, slot)], memb.at[item], m_send.at[item], m_recv.at[item], (0, place.d)
        )

    def one_item(item):
        @pl.when(s == 0)
        def _():
            pltpu.make_async_copy(x0_ref.at[item], xb.at[item], xsem.at[item]).wait()
            if segment > 0:

                @pl.when(c == 0)
                def _():
                    xb[item, :slot] = memory_ref[item]
                    xb[item, slot : 2 * slot] = memory_ref[item]

        @pl.when(s > 0)
        def _():
            handoff(item).wait_recv()

        if item == 0:
            weights[0].wait()
        for k in range(2 * D // STEP):
            kvb[item, own, k * STEP : (k + 1) * STEP] = dot(
                xb[item], vqkv[:, D + k * STEP : D + (k + 1) * STEP]
            ).astype(BF)
        exchange = remote(
            kvb.at[item, own], kvb.at[item, own], kv_send.at[item], kv_recv.at[item], (s, place.other)
        )
        exchange.start()
        for k in range(D // STEP):
            qb[item, :, k * STEP : (k + 1) * STEP] = dot(
                xb[item], vqkv[:, k * STEP : (k + 1) * STEP]
            ).astype(BF)
        bias = key_bias(geometry, segment, lens_ref[item, :1, :1])
        exchange.wait_recv()
        for pair in range(PAIRS):
            span = slice(pair * WIDE, (pair + 1) * WIDE)
            pair_probs(qb[item, :, span], kvb[item, :, span], bias, s_tmp.at[pair % 2], p_tmp.at[pair % 2])
            values = kvb[item, :, D + pair * WIDE : D + (pair + 1) * WIDE]
            attb[item, :, span] = folded_pair(dot(p_tmp[pair % 2], values)).astype(BF)
        if item == 0:
            weights[1].wait()
        for k in range(D // STEP):
            span = slice(k * STEP, (k + 1) * STEP)
            s1b[item, :, span] = xb[item, :, span].astype(F32) + dot(attb[item], vproj[:, span])
        for span in row_blocks(half):
            z, _ = normalized(s1b[item, span, :])
            normed = z * gain_one[...] + shift_one[...]
            nf[span, :] = normed
            nbb[item, span, :] = normed.astype(BF)
        if item == 0:
            weights[2].wait()
        for k in range(FF // STEP):
            span = slice(k * STEP, (k + 1) * STEP)
            pre = dot(nbb[item], vin[:, span]) + b_in[:, span]
            preb[:, span] = pre
            actb[item, :, span] = (0.5 * pre * (1.0 + lax.erf(pre * 0.7071067811865476))).astype(BF)
        if item == 0:
            weights[3].wait()
        for k in range(D // STEP):
            span = slice(k * STEP, (k + 1) * STEP)
            s2b[item, :, span] = nf[:, span] + dot(actb[item], vdown[:, span])
        for span in row_blocks(half):
            z, _ = normalized(s2b[item, span, :])
            hb[item, span, :] = (z * gain_two[...] + shift_two[...]).astype(BF)

        @pl.when(s < last)
        def _():
            handoff(item).start()

        if segment == 0:

            @pl.when((s == last) & (c == 0))
            def _():
                memory_move(item).start()

        for start in range(0, half, BLOCK):
            span = pl.ds(start, BLOCK)
            pre = preb[span, :]
            density = jnp.exp(-0.5 * pre * pre) * 0.3989422804014327
            slope = 0.5 * (1.0 + lax.erf(pre * 0.7071067811865476)) + pre * density
            gpb[item, span, :] = slope.astype(BF)
        for copy in outgoing(item):
            copy.start()
        exchange.wait_send()

    one_item(0)
    one_item(1)

    for item in range(2):

        @pl.when(s < last)
        def _():
            handoff(item).wait_send()

        if segment == 0:

            @pl.when((s == last) & (c == 0))
            def _():
                memory_move(item).wait_send()

            @pl.when((s == 0) & (c == 0))
            def _():
                memory_move(item).wait_recv()
                out = pltpu.make_async_copy(memb.at[item], o_mem.at[item], xsem.at[item])
                out.start()
                out.wait()

        for copy in outgoing(item):
            copy.wait()


def forward(segment, sections, geometry, collective, x0, memory, lens, weights):
    mem, slot, tok, rows = geometry
    half = rows // 2

    def pair(width, kind, height=half):
        return jax.ShapeDtypeStruct((2, height, width), kind)

    outs = (
        pair(D, BF),
        pair(D, BF),
        pair(2 * D, BF, rows),
        pair(D, BF),
        pair(D, BF),
        pair(FF, BF),
        pair(FF, BF),
        pair(D, F32),
        pair(D, F32),
        pair(D, BF),
        pair(D, BF, slot),
    )
    dma = pltpu.SemaphoreType.DMA
    return pl.pallas_call(
        functools.partial(forward_kernel, segment, sections, geometry),
        name="forward_layer",
        out_shape=outs,
        in_specs=[ANY, VMEM, VMEM] + [ANY] * 4 + [VMEM] * 5,
        out_specs=(ANY,) * len(outs),
        scratch_shapes=[
            pltpu.VMEM((D, 3 * D), BF),
            pltpu.VMEM((D, D), BF),
            pltpu.VMEM((D, FF), BF),
            pltpu.VMEM((FF, D), BF),
            pltpu.VMEM((2, half, D), BF),
            pltpu.VMEM((2, half, D), BF),
            pltpu.VMEM((2, rows, 2 * D), BF),
            pltpu.VMEM((2, half, D), BF),
            pltpu.VMEM((2, half, D), BF),
            pltpu.VMEM((2, half, FF), BF),
            pltpu.VMEM((2, half, FF), BF),
            pltpu.VMEM((half, FF), F32),
            pltpu.VMEM((2, half, D), F32),
            pltpu.VMEM((2, half, D), F32),
            pltpu.VMEM((2, half, D), BF),
            pltpu.VMEM((half, D), F32),
            pltpu.VMEM((2, slot, D), BF),
            pltpu.VMEM((2, rows, rows), F32),
            pltpu.VMEM((2, rows, rows), BF),
            dma((4,)),
            dma((2,)),
            dma((2, 10)),
            dma((2,)),
            dma((2,)),
            dma((2,)),
            dma((2,)),
            dma((2,)),
            dma((2,)),
        ],
        compiler_params=pltpu.CompilerParams(
            collective_id=collective, has_side_effects=True, vmem_limit_bytes=VMEM_LIMIT
        ),
    )(x0, memory, lens, *weights)


def backward_kernel(
    segment,
    sections,
    segments,
    geometry,
    g0_ref,
    carry_ref,
    lens_ref,
    r_q,
    r_kv,
    r_gp,
    r_s1,
    r_s2,
    w_qkv,
    w_proj,
    w_in,
    w_down,
    gain_one,
    gain_two,
    o_dpj,
    o_dbr,
    o_dpre,
    o_dfe,
    o_dx,
    o_mg,
    o_carry,
    o_small,
    vqkv,
    vproj,
    vin,
    vdown,
    gb,
    qb,
    kvb,
    gpb,
    z1b,
    z2b,
    r1b,
    r2b,
    pf,
    work,
    dsec,
    dfe,
    dpre,
    dbr,
    da,
    s_tmp,
    ds_tmp,
    dkv,
    dkv_in,
    dpj,
    dxb,
    mgb,
    carb,
    wsem,
    rsem,
    gsem,
    osem,
    kv_send,
    kv_recv,
    h_send,
    h_recv,
    m_send,
    m_recv,
):
    place = Place(sections)
    s, c = place.s, place.c
    mem, slot, tok, rows = geometry
    half = rows // 2
    own = pl.ds(pl.multiple_of(c * half, BLOCK), half)
    theirs = pl.ds(pl.multiple_of((1 - c) * half, BLOCK), half)
    last = sections - 1
    weights = [
        pltpu.make_async_copy(src, dst, wsem.at[k])
        for k, (src, dst) in enumerate(((w_down, vdown), (w_in, vin), (w_proj, vproj), (w_qkv, vqkv)))
    ]

    def residuals(item):
        pairs = ((r_q, qb), (r_kv, kvb), (r_s2, z2b), (r_gp, gpb), (r_s1, z1b))
        return [
            pltpu.make_async_copy(src.at[item], dst.at[item], rsem.at[item, k])
            for k, (src, dst) in enumerate(pairs)
        ]

    def seed_copy(item):
        return pltpu.make_async_copy(g0_ref.at[item], gb.at[item], gsem.at[item])

    for item in range(2):
        for copy in residuals(item):
            copy.start()
        if item == 0:
            for copy in weights:
                copy.start()
        pl.when(s == last)(seed_copy(item).start)
    o_small[...] = jnp.zeros_like(o_small)

    barrier = pltpu.get_barrier_semaphore()
    pl.semaphore_signal(barrier, inc=1, device_id=(place.next, place.d), device_id_type=MESH)
    pl.semaphore_signal(barrier, inc=1, device_id=(s, place.other), device_id_type=MESH)
    pl.semaphore_wait(barrier, 2)

    def outgoing(item):
        pairs = (
            (dpj, o_dpj),
            (dbr, o_dbr),
            (dpre, o_dpre),
            (dfe, o_dfe),
            (dxb.at[item], o_dx),
        )
        return [
            pltpu.make_async_copy(src, dst.at[item], osem.at[item, k])
            for k, (src, dst) in enumerate(pairs)
        ]

    def handoff(item):
        return remote(dxb.at[item], gb.at[item], h_send.at[item], h_recv.at[item], (place.prev, place.d))

    def carry_move(item):
        return remote(mgb.at[item], carb.at[item], m_send.at[item], m_recv.at[item], (last, place.d))

    def prologue(item):
        for copy in residuals(item):
            copy.wait()
        bias = key_bias(geometry, segment, lens_ref[item, :1, :1])
        for z_ref, r_ref in ((z2b, r2b), (z1b, r1b)):
            for span in row_blocks(half):
                z, scale = normalized(z_ref[item, span, :])
                z_ref[item, span, :] = z
                r_ref[item, span, :] = jnp.broadcast_to(scale, (BLOCK, 128))
        for pair in range(PAIRS):
            span = slice(pair * WIDE, (pair + 1) * WIDE)
            pair_probs(
                qb[item, :, span], kvb[item, :, span], bias, s_tmp.at[pair % 2], pf, (item, pair)
            )

    def norm_back(g, z, scale, gain):
        scaled = g * gain
        mean_u = jnp.mean(scaled, axis=-1, keepdims=True)
        mean_uz = jnp.mean(scaled * z, axis=-1, keepdims=True)
        return (scaled - mean_u - z * mean_uz) * scale

    def folded_rows(value):
        return value[: BLOCK // 2] + value[BLOCK // 2 :]

    def main(item):
        @pl.when(s == last)
        def _():
            seed_copy(item).wait()
            length = lens_ref[item, :1, :1]
            for index, span in enumerate(row_blocks(half)):
                row = c * half + index * BLOCK + lax.broadcasted_iota(jnp.int32, (BLOCK, D), 0)
                position = row - 2 * slot + segment * tok
                valid = (row >= 2 * slot) & (position.astype(F32) < length)
                work[span, :] = jnp.where(valid, gb[item, span, :].astype(F32), 0.0)
            if segment < segments - 1:

                @pl.when(c == 0)
                def _():
                    work[slot : 2 * slot, :] = carry_ref[item]

        @pl.when(s < last)
        def _():
            handoff(item).wait_recv()
            for span in row_blocks(half):
                work[span, :] = gb[item, span, :].astype(F32)

        if item > 0:
            for copy in outgoing(item - 1):
                copy.wait()
        gain_sum = jnp.zeros((BLOCK // 2, D), F32)
        shift_sum = jnp.zeros((BLOCK // 2, D), F32)
        for span in row_blocks(half):
            g = work[span, :]
            z = z2b[item, span, :]
            back = norm_back(g, z, r2b[item, span, :1], gain_two[...])
            dsec[span, :] = back
            dfe[span, :] = back.astype(BF)
            gain_sum += folded_rows(g * z)
            shift_sum += folded_rows(g)
        o_small[2:3, :] += jnp.sum(gain_sum, axis=0, keepdims=True)
        o_small[3:4, :] += jnp.sum(shift_sum, axis=0, keepdims=True)
        if item == 0:
            weights[0].wait()
        for k in range(FF // STEP):
            span = slice(k * STEP, (k + 1) * STEP)
            pre = (dot_nt(dfe[...], vdown[span, :]) * gpb[item, :, span].astype(F32)).astype(BF)
            dpre[:, span] = pre
            start = (k * STEP) % D
            row = 4 + (k * STEP) // D
            o_small[row : row + 1, start : start + STEP] += jnp.sum(pre.astype(F32), axis=0, keepdims=True)
        if item == 0:
            weights[1].wait()
        for k in range(D // STEP):
            span = slice(k * STEP, (k + 1) * STEP)
            work[:, span] = dsec[:, span] + dot_nt(dpre[...], vin[span, :])
        gain_sum = jnp.zeros((BLOCK // 2, D), F32)
        shift_sum = jnp.zeros((BLOCK // 2, D), F32)
        for span in row_blocks(half):
            g = work[span, :]
            z = z1b[item, span, :]
            back = norm_back(g, z, r1b[item, span, :1], gain_one[...])
            work[span, :] = back
            dbr[span, :] = back.astype(BF)
            gain_sum += folded_rows(g * z)
            shift_sum += folded_rows(g)
        o_small[0:1, :] += jnp.sum(gain_sum, axis=0, keepdims=True)
        o_small[1:2, :] += jnp.sum(shift_sum, axis=0, keepdims=True)
        if item == 0:
            weights[2].wait()
        for k in range(D // STEP):
            span = slice(k * STEP, (k + 1) * STEP)
            da[:, span] = dot_nt(dbr[...], vproj[span, :]).astype(BF)
        sends = []
        for pair in range(PAIRS):
            span = slice(pair * WIDE, (pair + 1) * WIDE)
            keys = kvb[item, :, span]
            values = kvb[item, :, D + pair * WIDE : D + (pair + 1) * WIDE]
            da2 = stacked_pair(da[:, span])
            q2 = stacked_pair(qb[item, :, span] * jnp.asarray(HEAD**-0.5, BF))
            dp_ref = s_tmp.at[pair % 2]
            ds_ref = ds_tmp.at[pair % 2]
            dp_ref[...] = dot_nt(da2, values)
            for start in range(0, rows, 2 * BLOCK):
                block = pl.ds(start, 2 * BLOCK)
                probs = pf[item, pair, block, :].astype(F32)
                grads = dp_ref[block, :]
                total = jnp.sum(probs * grads, axis=-1, keepdims=True)
                ds_ref[block, :] = (probs * (grads - total)).astype(BF)
            dkv[pair, :, :WIDE] = dot_tn(ds_ref[...], q2)
            dkv[pair, :, WIDE:] = dot_tn(pf[item, pair], da2)
            move = remote(
                dkv.at[pair, theirs],
                dkv_in.at[item, pair],
                kv_send.at[item, pair],
                kv_recv.at[item, pair],
                (s, place.other),
            )
            move.start()
            sends.append(move)
            dpj[:, span] = (folded_pair(dot(ds_ref[...], keys)) * HEAD**-0.5).astype(BF)
        if item == 0:
            weights[3].wait()
        for pair in range(PAIRS):
            sends[pair].wait_recv()
            for part in range(2):
                start = (part + 1) * D + pair * WIDE
                lanes = slice(part * WIDE, (part + 1) * WIDE)
                dpj[:, start : start + WIDE] = (
                    dkv[pair, own, lanes] + dkv_in[item, pair, :, lanes]
                ).astype(BF)
        for k in range(D // STEP):
            span = slice(k * STEP, (k + 1) * STEP)
            dxb[item, :, span] = (work[:, span] + dot_nt(dpj[...], vqkv[span, :])).astype(BF)

        pl.when(s > 0)(handoff(item).start)

        @pl.when((s == 0) & (c == 0))
        def _():
            mgb[item] = dxb[item, :slot].astype(F32) + dxb[item, slot : 2 * slot].astype(F32)
            if segment > 0:
                carry_move(item).start()

        for copy in outgoing(item):
            copy.start()
        for move in sends:
            move.wait_send()

    prologue(0)
    pl.when(s < last)(functools.partial(prologue, 1))
    main(0)
    pl.when(s == last)(functools.partial(prologue, 1))
    main(1)

    for item in range(2):
        pl.when(s > 0)(handoff(item).wait_send)
        if item == 1:
            for copy in outgoing(item):
                copy.wait()

        @pl.when((s == 0) & (c == 0))
        def _():
            out = pltpu.make_async_copy(mgb.at[item], o_mg.at[item], gsem.at[item])
            out.start()
            out.wait()
            if segment > 0:
                carry_move(item).wait_send()

        if segment > 0:

            @pl.when((s == last) & (c == 0))
            def _():
                carry_move(item).wait_recv()
                out = pltpu.make_async_copy(carb.at[item], o_carry.at[item], gsem.at[item])
                out.start()
                out.wait()


def backward(segment, sections, segments, geometry, collective, g0, carry, lens, kept, weights):
    mem, slot, tok, rows = geometry
    half = rows // 2

    def pair(width, kind, height=half):
        return jax.ShapeDtypeStruct((2, height, width), kind)

    outs = (
        pair(3 * D, BF),
        pair(D, BF),
        pair(FF, BF),
        pair(D, BF),
        pair(D, BF),
        pair(D, F32, slot),
        pair(D, F32, slot),
        jax.ShapeDtypeStruct((8, D), F32),
    )
    dma = pltpu.SemaphoreType.DMA
    return pl.pallas_call(
        functools.partial(backward_kernel, segment, sections, segments, geometry),
        name="backward_layer",
        out_shape=outs,
        in_specs=[ANY, VMEM, VMEM] + [ANY] * 5 + [ANY] * 4 + [VMEM] * 2,
        out_specs=(ANY,) * 7 + (VMEM,),
        scratch_shapes=[
            pltpu.VMEM((D, 3 * D), BF),
            pltpu.VMEM((D, D), BF),
            pltpu.VMEM((D, FF), BF),
            pltpu.VMEM((FF, D), BF),
            pltpu.VMEM((2, half, D), BF),
            pltpu.VMEM((2, half, D), BF),
            pltpu.VMEM((2, rows, 2 * D), BF),
            pltpu.VMEM((2, half, FF), BF),
            pltpu.VMEM((2, half, D), F32),
            pltpu.VMEM((2, half, D), F32),
            pltpu.VMEM((2, half, 128), F32),
            pltpu.VMEM((2, half, 128), F32),
            pltpu.VMEM((2, PAIRS, rows, rows), BF),
            pltpu.VMEM((half, D), F32),
            pltpu.VMEM((half, D), F32),
            pltpu.VMEM((half, D), BF),
            pltpu.VMEM((half, FF), BF),
            pltpu.VMEM((half, D), BF),
            pltpu.VMEM((half, D), BF),
            pltpu.VMEM((2, rows, rows), F32),
            pltpu.VMEM((2, rows, rows), BF),
            pltpu.VMEM((PAIRS, rows, 2 * WIDE), F32),
            pltpu.VMEM((2, PAIRS, half, 2 * WIDE), F32),
            pltpu.VMEM((half, 3 * D), BF),
            pltpu.VMEM((2, half, D), BF),
            pltpu.VMEM((2, slot, D), F32),
            pltpu.VMEM((2, slot, D), F32),
            dma((4,)),
            dma((2, 5)),
            dma((2,)),
            dma((2, 5)),
            dma((2, PAIRS)),
            dma((2, PAIRS)),
            dma((2,)),
            dma((2,)),
            dma((2,)),
            dma((2,)),
        ],
        compiler_params=pltpu.CompilerParams(
            collective_id=collective, has_side_effects=True, vmem_limit_bytes=VMEM_LIMIT
        ),
    )(g0, carry, lens, *kept, *weights)


def on_device(
    sections,
    inputs,
    out_grad,
    memory,
    lengths,
    w_qkv,
    w_proj,
    gain_one,
    shift_one,
    w_in,
    b_in,
    w_down,
    gain_two,
    shift_two,
):
    segs, tok, part = inputs.shape[1:]
    mem = memory.shape[1]
    slot = -(-mem // BLOCK) * BLOCK
    rows = -(-(2 * slot + tok) // (2 * BLOCK)) * 2 * BLOCK
    half = rows // 2
    geometry = (mem, slot, tok, rows)
    back_pad = rows - 2 * slot - tok

    def in_slots(array):
        return jnp.pad(array, ((0, 0), (2 * slot, back_pad), (0, 0)))

    def halves(array):
        return array.reshape(segs, 2, half, part).transpose(1, 0, 2, 3)

    tokens = in_slots(inputs[0])
    tokens = tokens.at[0, :mem].set(memory[0]).at[0, slot : slot + mem].set(memory[0])
    cotangent = in_slots(out_grad[0])
    length_tile = jnp.broadcast_to(lengths.astype(F32), (8, 128))
    x_all, g_all, lens = spread(sections, halves(tokens), halves(cotangent), length_tile)

    def of_segment(array, segment):
        return array[:, :, segment].transpose(0, 2, 1, 3).reshape(2, half, D)

    matrices = (w_qkv[0], w_proj[0], w_in[0], w_down[0])
    forward_weights = matrices + (gain_one, shift_one, b_in, gain_two, shift_two)
    backward_weights = matrices + (gain_one, gain_two)
    carried = jnp.zeros((2, slot, D), BF)
    kept = []
    for segment in range(segs):
        kept.append(
            forward(
                segment, sections, geometry, 2 + segment, of_segment(x_all, segment), carried, lens, forward_weights
            )
        )
        carried = kept[-1][-1]
    grads = [None] * segs
    carry = jnp.zeros((2, slot, D), F32)
    for segment in reversed(range(segs)):
        x, q, kv, att, nb, act, gp, s1, s2, hid, _ = kept[segment]
        grads[segment] = backward(
            segment,
            sections,
            segs,
            geometry,
            2 + segs + segment,
            of_segment(g_all, segment),
            carry,
            lens,
            (q, kv, gp, s1, s2),
            backward_weights,
        )
        carry = grads[segment][6]

    def per_owner(arrays):
        stacked = jnp.stack(arrays, axis=1)
        return stacked.reshape(2, segs, half, sections, part).transpose(0, 3, 1, 2, 4)

    memory_term = grads[0][5].reshape(2, slot, sections, part).transpose(0, 2, 1, 3)
    out_parts, in_parts, memory_part = collect(
        sections, per_owner([k[9] for k in kept]), per_owner([g[4] for g in grads]), memory_term
    )

    def owned(parts):
        return parts.transpose(1, 0, 2, 3).reshape(segs, rows, part)[:, 2 * slot : 2 * slot + tok]

    position = jnp.arange(segs * tok, dtype=jnp.int32).reshape(segs, tok)
    token_valid = position < lengths[0]
    outputs = jnp.where(token_valid[:, :, None], owned(out_parts), jnp.zeros((), BF))
    input_grad = owned(in_parts)
    memory_grad = memory_part[:mem]

    def weight_grad(left, right):
        lefts = jnp.concatenate([k.reshape(2 * half, -1) for k in left])
        rights = jnp.concatenate([g.reshape(2 * half, -1) for g in right])
        full = jnp.einsum("rd,re->de", lefts, rights, preferred_element_type=F32)
        return lax.psum_scatter(full.astype(BF), "dp", scatter_dimension=0, tiled=True).astype(F32)

    def kept_of(index):
        return [k[index] for k in kept]

    def grad_of(index):
        return [g[index] for g in grads]

    d_qkv = weight_grad(kept_of(0), grad_of(0))
    d_proj = weight_grad(kept_of(3), grad_of(1))
    d_in = weight_grad(kept_of(4), grad_of(2))
    d_down = weight_grad(kept_of(5), grad_of(3))
    small = lax.psum(sum(g[7] for g in grads), "dp")
    devices = lax.axis_size("dp")
    index = lax.axis_index("dp")

    def vector(value):
        size = value.size // devices
        return lax.dynamic_slice_in_dim(value.reshape(-1), index * size, size, 0)[None]

    return (
        outputs[None],
        input_grad[None],
        memory_grad[None],
        d_qkv[None],
        d_proj[None],
        vector(small[0]),
        vector(small[1]),
        d_in[None],
        vector(small[4:8]),
        d_down[None],
        vector(small[2]),
        vector(small[3]),
    )


def solution(mesh):
    return jax.shard_map(
        functools.partial(on_device, mesh.shape["section"]),
        mesh=mesh,
        in_specs=(
            P("dp", None, None, "section"),
            P("dp", None, None, "section"),
            P("dp", None, "section"),
            P("dp"),
            P("section", None, None),
            P("section", None, None),
            P("section", None),
            P("section", None),
            P("section", None, None),
            P("section", None),
            P("section", None, None),
            P("section", None),
            P("section", None),
        ),
        out_specs=(
            P("dp", None, None, "section"),
            P("dp", None, None, "section"),
            P("dp", None, "section"),
            P("section", "dp", None),
            P("section", "dp", None),
            P("section", "dp"),
            P("section", "dp"),
            P("section", "dp", None),
            P("section", "dp"),
            P("section", "dp", None),
            P("section", "dp"),
            P("section", "dp"),
        ),
        check_vma=False,
    )
```

time: 2730 us -> 734 us (0.27)
  waiting for transfers between devices: 1100 us -> 68.4 us
  starting transfers between devices: 952 us -> 0.42 us
  Pallas kernels: 0 us -> 515 us
  matrix products: 304 us -> 33.4 us
  other arithmetic: 156 us -> 15.6 us
  local copies, waits for them, and re-layouts: 142 us -> 50.7 us
  loops' own time: 47.8 us -> 0 us
    ppermute x15 -> x0, starting transfers between devices: 951 us -> none  [shifted(): lax.ppermute(value, axis, [(i, (i + by) % devices) for i in range(devices)])]
    ppermute x15 -> x0, waiting for transfers between devices: 550 us -> none  [shifted(): lax.ppermute(value, axis, [(i, (i + by) % devices) for i in range(devices)])]
    pallas_call x0 -> x6, Pallas kernels: none -> 515 us  [the longest x2 317 us: backward(): pl.pallas_call(functools.partial(backward_kernel, segment, sections, segm...]
    dot_general x38 -> x4, matrix products: 304 us -> 33.4 us  [weight_grad(): full = jnp.einsum('rd,re->de', lefts, rights, preferred_element_type=F32)]
    reduce_scatter x4, waiting for transfers between devices: 318 us -> 68.3 us  [weight_grad(): lax.psum_scatter(full.astype(BF), 'dp', scatter_dimension=0, tiled=True)]
    unnamed x22 -> x4, waiting for transfers between devices: 213 us -> 0.07 us
    another operation x17 -> x0, loops' own time: 47.8 us -> none  [the longest x8 30.6 us: on_device(): lax.cond(is_live, run_section, pass_section, rows_in, kept_store, out_store)]
    reduce_sum x18 -> x0, other arithmetic: 44.9 us -> none  [the longest x2 18.1 us: attention_forward(): denominator = jnp.sum(exponent, axis=-1, keepdims=True)]
  transfers between devices with their start and end apart: 29 -> 4, of which waited for: 28 -> 2; matrix products, arithmetic and copies ran while one was open for 2% -> 8% of each run, Pallas kernels for 0% -> 4%
where the time goes in v1:
time: 734 us; the launch traced here: 728 us
  Pallas kernels  515 us (70%)
  waiting for transfers between devices  68.4 us (9%)
  local copies, waits for them, and re-layouts  50.7 us (7%)
  matrix products  33.4 us (5%)
  blocking collectives  29.6 us (4%)
  other arithmetic  15.6 us (2%)
  between operations  15.2 us (2%)
    pallas_call x2, Pallas kernels, backward(): pl.pallas_call(functools.partial(backward_kernel, segment, sections, segm...  317 us
    pallas_call x2, Pallas kernels, forward(): pl.pallas_call(functools.partial(forward_kernel, segment, sections, geome...  148 us
    reduce_scatter x4, waiting for transfers between devices, weight_grad(): lax.psum_scatter(full.astype(BF), 'dp', scatter_dimension=0, tiled=True)  68.3 us
    dot_general x4, matrix products, weight_grad(): full = jnp.einsum('rd,re->de', lefts, rights, preferred_element_type=F32)  33.4 us
    psum x1, blocking collectives, on_device(): small = lax.psum(sum((g[7] for g in grads)), 'dp')  29.6 us
    pallas_call x1, Pallas kernels, collect(): pl.pallas_call(functools.partial(collect_kernel, sections), name='collect...  26 us
    pallas_call x1, Pallas kernels, spread(): pl.pallas_call(functools.partial(spread_kernel, sections), name='spread_i...  23.9 us
  transfers between devices with their start and end apart: 4, of which 2 were waited for; matrix products, arithmetic and copies ran while one was open for 8% of the time, Pallas kernels for 4%

profile of v1, /device:TPU:0, one launch (start us, length us, event | category | flops | bytes accessed | tf_op | source)
XLA Modules:
  0.0 728.3 jit_solution(9109942994557487761)
XLA Ops:
  7.2 0.6 fusion.44
  7.8 1.2 copy.31
  9.1 1.4 and_reduce_fusion
  10.5 0.8 scatter.6
  11.3 2.7 dynamic-slice_select_fusion
  14.0 1.5 scatter.9
  15.5 0.8 copy.53
  17.0 0.2 copy.33
  17.3 0.8 copy.52
  18.1 0.6 broadcast_in_dim.65.len_ref
  18.7 23.9 %spread_items.1 = (bf16[2,4,2,272,192]{4,3,2,1,0:T(8,128)(2,1)}, bf16[2,4,2,272,192]{4,3,2,1,0:T(8,128)(2,1)}, f32[2,8,128]{2,1,0:T(8,128)}) custom-call(bf16[2,2,272,192]{3,2,1,0:T(8,128)(2,1)} %bitcast.97, bf16[2,2,272,192]{3,2,1,0:T(8,128)(2,1)} %bitcast.98, f32[8,128]{1,0:T(8,128)} %broadcast_in_dim.65.len_ref), custom_call_target="tpu_custom_call" | custom-call | tf_op jit(solution)/shard_map/spread_items/pallas_call | solution.py:119
  42.6 2.6 slice_bitcast_fusion.1
  45.2 1.6 copy.35
  46.8 3.1 reshape.214.x0_ref
  49.8 1.6 copy.36
  51.4 3.3 reshape.215.x0_ref
  54.7 0.6 copy.40
  55.3 1.9 reshape.217.g0_ref
  57.2 0.6 copy.39
  57.8 1.9 reshape.216.g0_ref
  59.7 0.6 broadcast_in_dim.66.memory_ref
  60.3 109.4 %forward_layer.2 = (bf16[2,272,768]{2,1,0:T(8,128)(2,1)}, bf16[2,272,768]{2,1,0:T(8,128)(2,1)}, bf16[2,544,1536]{2,1,0:T(8,128)(2,1)}, bf16[2,272,768]{2,1,0:T(8...) custom-call(bf16[2,272,768]{2,1,0:T(8,128)(2,1)} %reshape.214.x0_ref, ...), custom_call_target="tpu_custom_call" | custom-call | tf_op jit(solution)/shard_map/forward_layer/pallas_call | solution.py:507
  169.7 38.8 %forward_layer.3 = (bf16[2,272,768]{2,1,0:T(8,128)(2,1)}, bf16[2,272,768]{2,1,0:T(8,128)(2,1)}, bf16[2,544,1536]{2,1,0:T(8,128)(2,1)}, bf16[2,272,768]{2,1,0:T(8...) custom-call(bf16[2,272,768]{2,1,0:T(8,128)(2,1)} %reshape.215.x0_ref, ...), custom_call_target="tpu_custom_call" | custom-call | tf_op jit(solution)/shard_map/forward_layer/pallas_call | solution.py:507
  208.5 0.6 broadcast_in_dim.67.carry_ref
  209.1 189.9 %backward_layer.2 = (bf16[2,272,2304]{2,1,0:T(8,128)(2,1)}, bf16[2,272,768]{2,1,0:T(8,128)(2,1)}, bf16[2,272,3072]{2,1,0:T(8,128)(2,1)}, bf16[2,272,768]{2,1,0:T...) custom-call(bf16[2,272,768]{2,1,0:T(8,128)(2,1)} %reshape.217.g0_ref, ...), custom_call_target="tpu_custom_call" | custom-call | tf_op jit(solution)/shard_map/backward_layer/pallas_call | solution.py:864
  399.0 127.0 %backward_layer.3 = (bf16[2,272,2304]{2,1,0:T(8,128)(2,1)}, bf16[2,272,768]{2,1,0:T(8,128)(2,1)}, bf16[2,272,3072]{2,1,0:T(8,128)(2,1)}, bf16[2,272,768]{2,1,0:T...) custom-call(bf16[2,272,768]{2,1,0:T(8,128)(2,1)} %reshape.216.g0_ref, ...), custom_call_target="tpu_custom_call" | custom-call | tf_op jit(solution)/shard_map/backward_layer/pallas_call | solution.py:864
  526.1 4.8 fusion.33
  531.0 8.6 %convolution_convert_fusion = bf16[768,2304]{1,0:T(8,128)(2,1)} fusion(bf16[544,2304]{1,0:T(8,128)(2,1)S(1)} %bitcast.111, bf16[544,2304]{1,0:T(8,128)(2,1)} %bitcast.112, bf16[544,768]{1,0:T(8,128)(2,1)} %bitcast.117, bf16[544,768]{1,0:T(8,128)(2,1)S(1)} %bitcast.115), kind=kOutput, calls=%fused_computation.10 | convolution fusion | flops 3865509888 | bytes 10223616 | tf_op jit(solution)/shard_map/rd,re->de/dot_general | solution.py:1005
  539.7 1.9 copy-done.7
  541.5 10.0 %fusion.8 = bf16[3072,768]{1,0:T(8,128)(2,1)} fusion(bf16[544,3072]{1,0:T(8,128)(2,1)} %bitcast.109, bf16[544,3072]{1,0:T(8,128)(2,1)S(1)} %bitcast.107, bf16[544,768]{1,0:T(8,128)(2,1)} %bitcast.116, bf16[544,768]{1,0:T(8,128)(2,1)} %bitcast.119), kind=kOutput, calls=%fused_computation.8 | convolution fusion | flops 5152899072 | bytes 13074432 | tf_op jit(solution)/shard_map/rd,re->de/dot_general | solution.py:1005
  551.5 0.3 reduce-scatter.9.cloned.1.call-start
  551.8 1.6 copy-done.8
  553.4 10.0 %fusion.11 = bf16[768,3072]{1,0:T(8,128)(2,1)} fusion(bf16[544,3072]{1,0:T(8,128)(2,1)S(1)} %bitcast.108, bf16[544,3072]{1,0:T(8,128)(2,1)} %bitcast.110, bf16[544,768]{1,0:T(8,128)(2,1)} %bitcast.114, bf16[544,768]{1,0:T(8,128)(2,1)} %bitcast.113), kind=kOutput, calls=%fused_computation.9 | convolution fusion | flops 5152899072 | bytes 13074432 | tf_op jit(solution)/shard_map/rd,re->de/dot_general | solution.py:1005
  563.5 0.7 copy-done.4
  564.2 29.6 %psum.7 = f32[8,768]{1,0:T(8,128)S(1)} all-reduce(f32[8,768]{1,0:T(8,128)S(1)} %add.35), channel_id=1, replica_groups=mesh['section'=4,'dp'=8] {'dp'}, use_global_device_ids=true, to_apply=%region_3.4 | all-reduce | flops 6144 | bytes 49152 | tf_op jit(solution)/shard_map/psum | solution.py:1018
  593.9 0.6 broadcast_in_dim.78
  594.5 0.9 stack.21
  595.4 0.1 copy.41
  595.6 2.8 stack.22
  598.4 0.1 copy.42
  598.6 0.1 reshape.218
  598.7 0.7 copy.54
  599.4 3.5 stack.19
  602.9 1.4 copy.38
  604.3 3.5 stack.18
  607.9 1.4 copy.37
  609.3 1.7 maximum_bitcast_fusion.1.x_ref
  611.0 1.7 maximum_bitcast_fusion.h_ref
  612.7 26.0 %collect_results.1 = (bf16[2,2,272,192]{3,2,1,0:T(8,128)(2,1)}, bf16[2,2,272,192]{3,2,1,0:T(8,128)(2,1)}, f32[16,192]{1,0:T(8,128)}) custom-call(bf16[2,4,2,272,192]{4,3,2,1,0:T(8,128)(2,1)} %maximum_bitcast_fusion.h_ref, bf16[2,4,2,272,192]{4,3,2,1,0:T(8,128)(2,1)} %maximum_bitcast_fusion.1.x_ref, f32[2,4,16,192]{3,2,1,0:T(8,128)} %bitcast.106), custom_call_target="tpu_custom_call" | custom-call | tf_op jit(solution)/shard_map/collect_results/pallas_call | solution.py:207
  638.7 1.1 copy.44
  639.8 0.2 fusion.38
  640.1 0.9 copy.46
  641.1 0.9 copy.47
  642.0 0.6 copy.48
  642.7 0.6 constant_dynamic-slice_fusion
  643.2 0.6 constant_dynamic-slice_fusion.1
  643.8 0.6 constant_dynamic-slice_fusion.2
  644.4 0.6 constant_dynamic-slice_fusion.3
  645.0 1.6 bitcast_convert_fusion.3
  646.6 2.0 bitcast_convert_fusion.2
  648.6 14.9 %reduce-scatter.11.cloned.1.call-done = bf16[384,768]{1,0:T(8,128)(2,1)} async-done(((bf16[3072,768]{1,0:T(8,128)(2,1)}), bf16[384,768]{1,0:T(8,128)(2,1)}) %reduce-scatter.11.cloned.1.call-update) | async-done | bytes 589840 | tf_op jit(solution)/shard_map/reduce_scatter | solution.py:1006
  663.5 2.2 bitcast_convert_fusion
  665.7 53.5 %reduce-scatter.9.cloned.1.call-done = bf16[96,3072]{1,0:T(8,128)(2,1)} async-done(((bf16[768,3072]{1,0:T(8,128)(2,1)}), bf16[96,3072]{1,0:T(8,128)(2,1)}) %reduce-scatter.9.cloned.1.call-update) | async-done | bytes 589840 | tf_op jit(solution)/shard_map/reduce_scatter | solution.py:1006
  719.1 2.2 bitcast_convert_fusion.1
  (40 shorter events, 0.6 us)
Async XLA Ops:
  7.2 9.8 %copy-start.2 = (bf16[1,2,502,192]{2,3,1,0:T(8,128)(2,1)S(1)}, bf16[1,2,502,192]{2,3,1,0:T(8,128)(2,1)}, u32[]{:S(2)}) copy-start(bf16[1,2,502,192]{2,3,1,0:T(8,128)(2,1)} %param.18) | copy-start | bytes 1156612
  7.2 637.8 %reduce-scatter.7.cloned.1.call-start = ((), (), s32[]{:S(2)}) async-start(), calls=%async_computation.5 | async-start | bytes 1327104 | tf_op jit(solution)/shard_map/reduce_scatter | solution.py:1006
  526.1 4.9 copy-start.9
  526.1 4.9 copy-start.10
  530.9 115.7 %reduce-scatter.5.cloned.1.call-start = ((), (), s32[]{:S(2)}) async-start(), calls=%async_computation.4 | async-start | bytes 3981312 | tf_op jit(solution)/shard_map/reduce_scatter | solution.py:1006
  539.6 1.9 copy-start.7
  539.6 123.9 %reduce-scatter.11.cloned.1.call-start = ((), (), s32[]{:S(2)}) async-start(), calls=%async_computation.7 | async-start | bytes 5308416 | tf_op jit(solution)/shard_map/reduce_scatter | solution.py:1006
  551.5 1.9 copy-start.8
  551.5 167.6 %reduce-scatter.9.cloned.1.call-start = ((), (), s32[]{:S(2)}) async-start(), calls=%async_computation.6 | async-start | bytes 5308416 | tf_op jit(solution)/shard_map/reduce_scatter | solution.py:1006
  563.5 0.7 copy-start.4
  563.5 0.8 copy-start.5
  563.5 31.0 %copy-start = (bf16[2,272,768]{2,1,0:T(8,128)(2,1)S(1)}, bf16[2,272,768]{2,1,0:T(8,128)(2,1)}, u32[]{:S(2)}) copy-start(bf16[2,272,768]{2,1,0:T(8,128)(2,1)} %get-tuple-element.94) | copy-start | bytes 2506756
  595.6 3.0 copy-start.3
  638.7 2.3 copy-start.1
  639.8 2.2 copy-start.6
Sparse Core Ops, SparseCore 0:
  531.0 32.2 reduce-scatter.6
  565.7 42.4 reduce-scatter.4
  610.6 52.8 reduce-scatter.10
  665.8 53.3 reduce-scatter.8

commit v2 on v1

v2 whole, which is shorter than its diff:
```python
import functools

import jax
import jax.numpy as jnp
from jax import lax
from jax.experimental import pallas as pl
from jax.experimental.pallas import tpu as pltpu
from jax.sharding import PartitionSpec as P

D = 768
H = 12
HEAD = 64
FF = 3072
PAIRS = H // 2
WIDE = 2 * HEAD
STEP = 256
BLOCK = 16
BF = jnp.bfloat16
F32 = jnp.float32
MESH = pl.DeviceIdType.MESH
ANY = pl.BlockSpec(memory_space=pl.ANY)
VMEM = pl.BlockSpec(memory_space=pltpu.VMEM)
VMEM_LIMIT = 63 * 1024 * 1024


def dot(a, b):
    return jnp.dot(a, b, preferred_element_type=F32)


def dot_nt(a, b):
    return lax.dot_general(a, b, (((1,), (1,)), ((), ())), preferred_element_type=F32)


def dot_tn(a, b):
    return lax.dot_general(a, b, (((0,), (0,)), ((), ())), preferred_element_type=F32)


def cols(index):
    return pl.ds(index * STEP, STEP)


def remote(src, dst, send, recv, target):
    return pltpu.make_async_remote_copy(
        src_ref=src, dst_ref=dst, send_sem=send, recv_sem=recv, device_id=target, device_id_type=MESH
    )


class Place:
    def __init__(self, sections):
        self.s = lax.axis_index("section")
        self.d = lax.axis_index("dp")
        self.c = lax.rem(self.d, 2)
        self.base = self.d - self.c
        self.other = self.base + 1 - self.c
        self.next = lax.rem(self.s + 1, sections)
        self.prev = lax.rem(self.s + sections - 1, sections)


def plane_barrier(place, sections):
    barrier = pltpu.get_barrier_semaphore()
    for section in range(sections):
        for core in range(2):

            @pl.when((place.s != section) | (place.c != core))
            def _():
                pl.semaphore_signal(
                    barrier, inc=1, device_id=(section, place.base + core), device_id_type=MESH
                )

    pl.semaphore_wait(barrier, 2 * sections - 1)


def spread_kernel(sections, a_ref, g_ref, len_ref, x_ref, gr_ref, lens_ref, send, got_x, got_g, got_l, local):
    place = Place(sections)
    s, c = place.s, place.c
    plane_barrier(place, sections)
    moves = []
    for core in range(2):
        for which, (src, dst, target, got) in enumerate(
            ((a_ref, x_ref, 0, got_x), (g_ref, gr_ref, sections - 1, got_g))
        ):
            here = (s == target) & (c == core)
            slot = 2 * which + core
            far = remote(
                src.at[core], dst.at[c, s], send.at[slot], got.at[c, s], (target, place.base + core)
            )
            near = pltpu.make_async_copy(src.at[core], dst.at[c, s], local.at[which])
            moves.append((here, far, near))
    for here, far, near in moves:
        pl.when(jnp.logical_not(here))(far.start)
        pl.when(here)(near.start)
    far_len = remote(len_ref, lens_ref.at[c], send.at[4], got_l.at[0], (s, place.other))
    near_len = pltpu.make_async_copy(len_ref, lens_ref.at[c], local.at[2])
    far_len.start()
    near_len.start()
    for here, far, near in moves:
        pl.when(jnp.logical_not(here))(far.wait_send)
        pl.when(here)(near.wait)
    for which, (src, dst, target, got) in enumerate(
        ((a_ref, x_ref, 0, got_x), (g_ref, gr_ref, sections - 1, got_g))
    ):
        for core in range(2):
            for section in range(sections):

                @pl.when((s == target) & ((c != core) | (s != section)))
                def _():
                    remote(
                        src.at[0], dst.at[core, section], send.at[0], got.at[core, section], (s, place.d)
                    ).wait_recv()

    far_len.wait_send()
    near_len.wait()
    remote(len_ref, lens_ref.at[1 - c], send.at[4], got_l.at[0], (s, place.other)).wait_recv()


def spread(sections, a, g, length_tile):
    half = a.shape[2]
    block = (2, sections) + a.shape[1:]
    return pl.pallas_call(
        functools.partial(spread_kernel, sections),
        name="spread_items",
        out_shape=(
            jax.ShapeDtypeStruct(block, BF),
            jax.ShapeDtypeStruct(block, BF),
            jax.ShapeDtypeStruct((2, 8, 128), F32),
        ),
        in_specs=[ANY, ANY, ANY],
        out_specs=(ANY, ANY, ANY),
        scratch_shapes=[
            pltpu.SemaphoreType.DMA((5,)),
            pltpu.SemaphoreType.DMA((2, sections)),
            pltpu.SemaphoreType.DMA((2, sections)),
            pltpu.SemaphoreType.DMA((1,)),
            pltpu.SemaphoreType.DMA((3,)),
        ],
        compiler_params=pltpu.CompilerParams(collective_id=0, has_side_effects=True),
    )(a, g, length_tile)


def collect_kernel(sections, h_ref, x_ref, m_ref, oh_ref, ox_ref, om_ref, send, got_h, got_x, got_m, local):
    place = Place(sections)
    s, c = place.s, place.c
    plane_barrier(place, sections)
    last = sections - 1
    jobs = (
        (h_ref, oh_ref, last, got_h, 0),
        (x_ref, ox_ref, 0, got_x, 1),
    )
    for src, dst, origin, got, which in jobs:
        for item in range(2):
            for section in range(sections):
                here = (s == section) & (c == item)
                mine = s == origin
                far = remote(
                    src.at[item, section], dst.at[c], send.at[which, item, section], got.at[c], (section, place.base + item)
                )
                near = pltpu.make_async_copy(src.at[item, section], dst.at[c], local.at[which])
                pl.when(mine & jnp.logical_not(here))(far.start)
                pl.when(mine & here)(near.start)
    for item in range(2):
        for section in range(sections):
            here = (s == section) & (c == item)
            mine = (s == 0) & (c == 0)
            far = remote(
                m_ref.at[item, section], om_ref, send.at[2, item, section], got_m.at[0], (section, place.base + item)
            )
            near = pltpu.make_async_copy(m_ref.at[item, section], om_ref, local.at[2])
            pl.when(mine & jnp.logical_not(here))(far.start)
            pl.when(mine & here)(near.start)
    for src, dst, origin, got, which in jobs:
        for item in range(2):
            for section in range(sections):
                here = (s == section) & (c == item)
                mine = s == origin
                far = remote(
                    src.at[item, section], dst.at[c], send.at[which, item, section], got.at[c], (section, place.base + item)
                )
                near = pltpu.make_async_copy(src.at[item, section], dst.at[c], local.at[which])
                pl.when(mine & jnp.logical_not(here))(far.wait_send)
                pl.when(mine & here)(near.wait)
        for core in range(2):

            @pl.when((s != origin) | (c != core))
            def _():
                remote(
                    src.at[0, 0], dst.at[core], send.at[which, 0, 0], got.at[core], (s, place.d)
                ).wait_recv()

    for item in range(2):
        for section in range(sections):
            here = (s == section) & (c == item)
            mine = (s == 0) & (c == 0)
            far = remote(
                m_ref.at[item, section], om_ref, send.at[2, item, section], got_m.at[0], (section, place.base + item)
            )
            near = pltpu.make_async_copy(m_ref.at[item, section], om_ref, local.at[2])
            pl.when(mine & jnp.logical_not(here))(far.wait_send)
            pl.when(mine & here)(near.wait)

    @pl.when((s != 0) | (c != 0))
    def _():
        remote(m_ref.at[0, 0], om_ref, send.at[2, 0, 0], got_m.at[0], (s, place.d)).wait_recv()


def collect(sections, h, x, m):
    block = (2,) + h.shape[2:]
    return pl.pallas_call(
        functools.partial(collect_kernel, sections),
        name="collect_results",
        out_shape=(
            jax.ShapeDtypeStruct(block, BF),
            jax.ShapeDtypeStruct(block, BF),
            jax.ShapeDtypeStruct(m.shape[2:], F32),
        ),
        in_specs=[ANY, ANY, ANY],
        out_specs=(ANY, ANY, ANY),
        scratch_shapes=[
            pltpu.SemaphoreType.DMA((3, 2, sections)),
            pltpu.SemaphoreType.DMA((2,)),
            pltpu.SemaphoreType.DMA((2,)),
            pltpu.SemaphoreType.DMA((1,)),
            pltpu.SemaphoreType.DMA((3,)),
        ],
        compiler_params=pltpu.CompilerParams(collective_id=1, has_side_effects=True),
    )(h, x, m)


def key_bias(geometry, segment, length, shape, dim):
    mem, slot, tok, rows = geometry
    row = lax.broadcasted_iota(jnp.int32, shape, dim)
    position = row - 2 * slot + segment * tok
    is_token = (row >= 2 * slot) & (row < 2 * slot + tok) & (position.astype(F32) < length)
    is_memory = (row < mem) | ((row >= slot) & (row < slot + mem))
    return jnp.where(is_token | is_memory, 0.0, -1e30)


def stacked_pair(pair):
    lane = lax.broadcasted_iota(jnp.int32, pair.shape, 1)
    zero = jnp.zeros_like(pair)
    return jnp.concatenate(
        [jnp.where(lane < HEAD, pair, zero), jnp.where(lane >= HEAD, pair, zero)], axis=0
    )


def folded_pair(both):
    half = both.shape[0] // 2
    lane = lax.broadcasted_iota(jnp.int32, (half, WIDE), 1)
    return jnp.where(lane < HEAD, both[:half], both[half:])


def scaled_queries(queries):
    return stacked_pair(queries * jnp.asarray(HEAD**-0.5, BF))


def normalized(rows):
    center = rows - jnp.mean(rows, axis=-1, keepdims=True)
    spread_of = jnp.mean(center * center, axis=-1, keepdims=True)
    scale = lax.rsqrt(spread_of + 1e-06)
    return center * scale, scale


def pieces(width, step=STEP):
    return [slice(start, start + step) for start in range(0, width, step)]


def row_chunks(half):
    first = half // 2 // BLOCK * BLOCK
    return ((0, first), (first, half - first))


def row_blocks(start, size):
    return [pl.ds(start + offset, BLOCK) for offset in range(0, size, BLOCK)]


def pair_span(pair, offset=0):
    return slice(offset + pair * WIDE, offset + (pair + 1) * WIDE)


def forward_kernel(
    sections,
    segments,
    geometry,
    x0_ref,
    lens_ref,
    w_qkv,
    w_proj,
    w_in,
    w_down,
    gain_one,
    shift_one,
    b_in,
    gain_two,
    shift_two,
    o_x,
    o_q,
    o_kv,
    o_att,
    o_nb,
    o_act,
    o_gp,
    o_s1,
    o_s2,
    o_hid,
    t_qkv,
    t_proj,
    t_in,
    t_down,
    vqkv,
    vproj,
    vin,
    vdown,
    xb,
    kvb,
    qb,
    attb,
    nbb,
    actb,
    gpb,
    s1b,
    s2b,
    hb,
    preb,
    nf,
    memb,
    s_tmp,
    probs,
    turned,
    wsem,
    xsem,
    osem,
    kv_send,
    kv_recv,
    h_send,
    h_recv,
    m_send,
    m_recv,
    tsem,
):
    place = Place(sections)
    s, c = place.s, place.c
    mem, slot, tok, rows = geometry
    half = rows // 2
    last = sections - 1
    steps = 2 * segments
    chunks = row_chunks(half)
    early = s >= 2
    weights = [
        pltpu.make_async_copy(src, dst, wsem.at[k])
        for k, (src, dst) in enumerate(((w_qkv, vqkv), (w_proj, vproj), (w_in, vin), (w_down, vdown)))
    ]

    @pl.when(s == 0)
    def _():
        for step in range(steps):
            pltpu.make_async_copy(x0_ref.at[step], xb.at[step], xsem.at[step]).start()

    for copy in weights:
        copy.start()
    barrier = pltpu.get_barrier_semaphore()
    pl.semaphore_signal(barrier, inc=1, device_id=(place.prev, place.d), device_id_type=MESH)
    pl.semaphore_signal(barrier, inc=1, device_id=(s, place.other), device_id_type=MESH)
    pl.semaphore_wait(barrier, 2)

    def outgoing(step):
        side = lax.rem(step, 2)
        pairs = (
            (xb.at[step], o_x),
            (kvb.at[step], o_kv),
            (qb.at[side], o_q),
            (attb.at[side], o_att),
            (nbb.at[side], o_nb),
            (actb.at[side], o_act),
            (gpb.at[side], o_gp),
            (s1b.at[side], o_s1),
            (s2b.at[side], o_s2),
            (hb.at[side], o_hid),
        )
        return [
            pltpu.make_async_copy(src, dst.at[step], osem.at[side, k])
            for k, (src, dst) in enumerate(pairs)
        ]

    def handoff(step, index):
        start, size = chunks[index]
        side = lax.rem(step, 2)
        span = pl.ds(start, size)
        return remote(
            hb.at[side, span],
            xb.at[step, span],
            h_send.at[side, index],
            h_recv.at[step, index],
            (place.next, place.d),
        )

    def memory_move(step):
        side = lax.rem(step, 2)
        return remote(
            hb.at[side, pl.ds(slot, slot)], memb.at[step], m_send.at[side], m_recv.at[step], (0, place.d)
        )

    def exchange(step, index):
        start, size = chunks[index]
        span = pl.ds(pl.multiple_of(c * half + start, BLOCK), size)
        return remote(
            kvb.at[step, span],
            kvb.at[step, span],
            kv_send.at[index],
            kv_recv.at[step, index],
            (s, place.other),
        )

    def settle(step):
        @pl.when(s < last)
        def _():
            for index in range(len(chunks)):
                handoff(step, index).wait_send()

        @pl.when((s == last) & (c == 0) & (step < steps - 2))
        def _():
            memory_move(step).wait_send()

        for copy in outgoing(step):
            copy.wait()

    def turn_weights():
        @pl.when(early)
        def _():
            for copy in weights:
                copy.wait()

        blocks = []
        for src, dst in ((vqkv, t_qkv), (vproj, t_proj), (vin, t_in), (vdown, t_down)):
            for block in range(src.shape[0] * src.shape[1] // (D * D)):
                span = pl.ds(block * D, D)
                if src.shape[0] == D:
                    blocks.append((src, (slice(None), span), dst.at[span]))
                else:
                    blocks.append((src, (span, slice(None)), dst.at[:, span]))
        moves = []
        for index, (src, where, dst) in enumerate(blocks):
            spot = index % 3
            if index >= 3:
                moves[index - 3].wait()
            turned[spot] = jnp.transpose(src[where])
            moves.append(pltpu.make_async_copy(turned.at[spot], dst, tsem.at[spot]))
            moves[-1].start()
        for move in moves[-3:]:
            move.wait()

    def one_step(step, state):
        pl.when(step == jnp.where(early, 0, steps))(turn_weights)
        pl.when(step < steps)(lambda: compute_step(step))
        return state

    def compute_step(step):
        side = lax.rem(step, 2)
        segment = lax.div(step, 2)
        first = (step == 0) & jnp.logical_not(early)

        @pl.when(s == 0)
        def _():
            pltpu.make_async_copy(x0_ref.at[step], xb.at[step], xsem.at[step]).wait()

            @pl.when((c == 0) & (step >= 2))
            def _():
                memory_move(step - 2).wait_recv()
                xb[step, :slot] = memb[step - 2]
                xb[step, slot : 2 * slot] = memb[step - 2]

        pl.when(step >= 2)(lambda: settle(step - 2))
        for index, (start, size) in enumerate(chunks):
            span = pl.ds(start, size)

            @pl.when(s > 0)
            def _():
                handoff(step, index).wait_recv()

            if index == 0:
                pl.when(first)(weights[0].wait)
            own = pl.ds(pl.multiple_of(c * half + start, BLOCK), size)
            for lanes in pieces(2 * D):
                kvb[step, own, lanes] = dot(
                    xb[step, span], vqkv[:, D + lanes.start : D + lanes.stop]
                ).astype(BF)
            exchange(step, index).start()
            for lanes in pieces(D):
                qb[side, span, lanes] = dot(xb[step, span], vqkv[:, lanes]).astype(BF)
        bias = key_bias(geometry, segment, lens_ref[side, :1, :1], (1, rows), 1)
        for index in range(len(chunks)):
            exchange(step, index).wait_recv()
        for index, (start, size) in enumerate(chunks):
            span = pl.ds(start, size)
            for pair in range(PAIRS):
                lanes = pair_span(pair)
                s_tmp[pair % 2, : 2 * size] = dot_nt(
                    scaled_queries(qb[side, span, lanes]), kvb[step, :, lanes]
                )
                for offset in range(0, 2 * size, 2 * BLOCK):
                    block = pl.ds(offset, 2 * BLOCK)
                    scores = s_tmp[pair % 2, block, :] + bias
                    exponent = jnp.exp(scores - jnp.max(scores, axis=-1, keepdims=True))
                    inverse = 1.0 / jnp.sum(exponent, axis=-1, keepdims=True)
                    probs[pair, block, :] = (exponent * inverse).astype(BF)
            for pair in range(PAIRS):
                mixed = dot(probs[pair, : 2 * size], kvb[step, :, pair_span(pair, D)])
                attb[side, span, pair_span(pair)] = folded_pair(mixed).astype(BF)
            if index == 0:
                pl.when(first)(weights[1].wait)
            for lanes in pieces(D):
                s1b[side, span, lanes] = xb[step, span, lanes].astype(F32) + dot(
                    attb[side, span], vproj[:, lanes]
                )
            for block in row_blocks(start, size):
                z, _ = normalized(s1b[side, block, :])
                normed = z * gain_one[...] + shift_one[...]
                nf[block, :] = normed
                nbb[side, block, :] = normed.astype(BF)
            if index == 0:
                pl.when(first)(weights[2].wait)
            for lanes in pieces(FF):
                pre = dot(nbb[side, span], vin[:, lanes]) + b_in[:, lanes]
                preb[span, lanes] = pre
                actb[side, span, lanes] = (
                    0.5 * pre * (1.0 + lax.erf(pre * 0.7071067811865476))
                ).astype(BF)
            if index == 0:
                pl.when(first)(weights[3].wait)
            for lanes in pieces(D):
                s2b[side, span, lanes] = nf[span, lanes] + dot(actb[side, span], vdown[:, lanes])
            for block in row_blocks(start, size):
                z, _ = normalized(s2b[side, block, :])
                hb[side, block, :] = (z * gain_two[...] + shift_two[...]).astype(BF)

            pl.when(s < last)(handoff(step, index).start)
            if index == 0:

                @pl.when((s == last) & (c == 0) & (step < steps - 2))
                def _():
                    memory_move(step).start()

        for block in row_blocks(0, half):
            pre = preb[block, :]
            density = jnp.exp(-0.5 * pre * pre) * 0.3989422804014327
            slope = 0.5 * (1.0 + lax.erf(pre * 0.7071067811865476)) + pre * density
            gpb[side, block, :] = slope.astype(BF)
        for copy in outgoing(step):
            copy.start()
        for index in range(len(chunks)):
            exchange(step, index).wait_send()

    lax.fori_loop(0, steps + 1, one_step, 0)
    settle(steps - 2)
    settle(steps - 1)


def forward(sections, segments, geometry, collective, x0, lens, weights):
    mem, slot, tok, rows = geometry
    half = rows // 2
    steps = 2 * segments

    def kept(width, kind, height=half):
        return jax.ShapeDtypeStruct((steps, height, width), kind)

    outs = (
        kept(D, BF),
        kept(D, BF),
        kept(2 * D, BF, rows),
        kept(D, BF),
        kept(D, BF),
        kept(FF, BF),
        kept(FF, BF),
        kept(D, F32),
        kept(D, F32),
        kept(D, BF),
        jax.ShapeDtypeStruct((3 * D, D), BF),
        jax.ShapeDtypeStruct((D, D), BF),
        jax.ShapeDtypeStruct((FF, D), BF),
        jax.ShapeDtypeStruct((D, FF), BF),
    )
    dma = pltpu.SemaphoreType.DMA
    return pl.pallas_call(
        functools.partial(forward_kernel, sections, segments, geometry),
        name="forward_layer",
        out_shape=outs,
        in_specs=[ANY, VMEM] + [ANY] * 4 + [VMEM] * 5,
        out_specs=(ANY,) * len(outs),
        scratch_shapes=[
            pltpu.VMEM((D, 3 * D), BF),
            pltpu.VMEM((D, D), BF),
            pltpu.VMEM((D, FF), BF),
            pltpu.VMEM((FF, D), BF),
            pltpu.VMEM((steps, half, D), BF),
            pltpu.VMEM((steps, rows, 2 * D), BF),
            pltpu.VMEM((2, half, D), BF),
            pltpu.VMEM((2, half, D), BF),
            pltpu.VMEM((2, half, D), BF),
            pltpu.VMEM((2, half, FF), BF),
            pltpu.VMEM((2, half, FF), BF),
            pltpu.VMEM((2, half, D), F32),
            pltpu.VMEM((2, half, D), F32),
            pltpu.VMEM((2, half, D), BF),
            pltpu.VMEM((half, FF), F32),
            pltpu.VMEM((half, D), F32),
            pltpu.VMEM((steps, slot, D), BF),
            pltpu.VMEM((2, rows, rows), F32),
            pltpu.VMEM((PAIRS, rows, rows), BF),
            pltpu.VMEM((3, D, D), BF),
            dma((4,)),
            dma((steps,)),
            dma((2, 10)),
            dma((2,)),
            dma((steps, 2)),
            dma((2, 2)),
            dma((steps, 2)),
            dma((2,)),
            dma((steps,)),
            dma((3,)),
        ],
        compiler_params=pltpu.CompilerParams(
            collective_id=collective, has_side_effects=True, vmem_limit_bytes=VMEM_LIMIT
        ),
    )(x0, lens, *weights)


def backward_kernel(
    sections,
    segments,
    geometry,
    g0_ref,
    lens_ref,
    r_q,
    r_kv,
    r_gp,
    r_s1,
    r_s2,
    w_qkv,
    w_proj,
    w_in,
    w_down,
    gain_one,
    gain_two,
    o_dpj,
    o_dbr,
    o_dpre,
    o_dfe,
    o_dx,
    o_mg,
    o_small,
    vqkv,
    vproj,
    vin,
    vdown,
    gb,
    qb,
    kvb,
    gpb,
    z1b,
    z2b,
    r1b,
    r2b,
    probs,
    work,
    dsec,
    dfe,
    dpre,
    dbr,
    da,
    dp_tmp,
    ds_tmp,
    dkv,
    dkv_in,
    dpj,
    dxb,
    mgb,
    carb,
    wsem,
    rsem,
    gsem,
    osem,
    kv_send,
    kv_recv,
    h_send,
    h_recv,
    m_send,
    m_recv,
):
    place = Place(sections)
    s, c = place.s, place.c
    mem, slot, tok, rows = geometry
    half = rows // 2
    own = pl.ds(pl.multiple_of(c * half, BLOCK), half)
    theirs = pl.ds(pl.multiple_of((1 - c) * half, BLOCK), half)
    last = sections - 1
    steps = 2 * segments
    chunks = row_chunks(half)
    weights = [
        pltpu.make_async_copy(src, dst, wsem.at[k])
        for k, (src, dst) in enumerate(((w_down, vdown), (w_in, vin), (w_proj, vproj), (w_qkv, vqkv)))
    ]

    def kept_index(step):
        return 2 * (segments - 1 - lax.div(step, 2)) + lax.rem(step, 2)

    def residuals(step):
        side = lax.rem(step, 2)
        pairs = ((r_q, qb), (r_kv, kvb), (r_s2, z2b), (r_gp, gpb), (r_s1, z1b))
        return [
            pltpu.make_async_copy(src.at[kept_index(step)], dst.at[side], rsem.at[side, k])
            for k, (src, dst) in enumerate(pairs)
        ]

    def seed_copy(step):
        return pltpu.make_async_copy(g0_ref.at[kept_index(step)], gb.at[step], gsem.at[step])

    for step in range(2):
        for copy in residuals(step):
            copy.start()
        if step == 0:
            for copy in weights:
                copy.start()

    @pl.when(s == last)
    def _():
        for step in range(steps):
            seed_copy(step).start()

    o_small[...] = jnp.zeros_like(o_small)
    barrier = pltpu.get_barrier_semaphore()
    pl.semaphore_signal(barrier, inc=1, device_id=(place.next, place.d), device_id_type=MESH)
    pl.semaphore_signal(barrier, inc=1, device_id=(s, place.other), device_id_type=MESH)
    pl.semaphore_wait(barrier, 2)

    def outgoing(step):
        pairs = (
            (dpj, o_dpj),
            (dbr, o_dbr),
            (dpre, o_dpre),
            (dfe, o_dfe),
        )
        return [
            pltpu.make_async_copy(src, dst.at[kept_index(step)], osem.at[k])
            for k, (src, dst) in enumerate(pairs)
        ]

    def outgoing_dx(step):
        side = lax.rem(step, 2)
        return pltpu.make_async_copy(dxb.at[side], o_dx.at[kept_index(step)], osem.at[4 + side])

    def outgoing_memory(step):
        return pltpu.make_async_copy(mgb.at[step], o_mg.at[lax.rem(step, 2)], gsem.at[step])

    def handoff(step, index):
        start, size = chunks[index]
        side = lax.rem(step, 2)
        span = pl.ds(start, size)
        return remote(
            dxb.at[side, span],
            gb.at[step, span],
            h_send.at[side, index],
            h_recv.at[step, index],
            (place.prev, place.d),
        )

    def carry_move(step):
        return remote(mgb.at[step], carb.at[step], m_send.at[step], m_recv.at[step], (last, place.d))

    def settle(step):
        @pl.when(s > 0)
        def _():
            for index in range(len(chunks)):
                handoff(step, index).wait_send()

        outgoing_dx(step).wait()

    def prologue(step):
        side = lax.rem(step, 2)
        segment = segments - 1 - lax.div(step, 2)
        for copy in residuals(step):
            copy.wait()
        for z_ref, r_ref in ((z2b, r2b), (z1b, r1b)):
            for block in row_blocks(0, half):
                z, scale = normalized(z_ref[side, block, :])
                z_ref[side, block, :] = z
                r_ref[side, block, :] = jnp.broadcast_to(scale, (BLOCK, 128))
        bias = key_bias(geometry, segment, lens_ref[side, :1, :1], (rows, 128), 0)
        for pair in range(PAIRS):
            lanes = pair_span(pair)
            keys = kvb[side, :, lanes]
            for start, size in chunks:
                queries = scaled_queries(qb[side, pl.ds(start, size), lanes])
                tiles = [bias] * (2 * size // 128)
                if 2 * size % 128:
                    tiles.append(bias[:, : 2 * size % 128])
                scores = dot_nt(keys, queries) + jnp.concatenate(tiles, axis=1)
                exponent = jnp.exp(scores - jnp.max(scores, axis=0, keepdims=True))
                inverse = 1.0 / jnp.sum(exponent, axis=0, keepdims=True)
                probs[side, pair, :, 2 * start : 2 * (start + size)] = (exponent * inverse).astype(BF)

    def norm_back(g, z, scale, gain):
        scaled = g * gain
        mean_u = jnp.mean(scaled, axis=-1, keepdims=True)
        mean_uz = jnp.mean(scaled * z, axis=-1, keepdims=True)
        return (scaled - mean_u - z * mean_uz) * scale

    def folded_rows(value):
        return value[: BLOCK // 2] + value[BLOCK // 2 :]

    def main(step):
        side = lax.rem(step, 2)
        segment = segments - 1 - lax.div(step, 2)
        first = step == 0
        pl.when(step >= 2)(lambda: settle(step - 2))

        @pl.when(step >= 1)
        def _():
            for copy in outgoing(step - 1):
                copy.wait()

        @pl.when(s == last)
        def _():
            seed_copy(step).wait()
            length = lens_ref[side, :1, :1]
            for index, block in enumerate(row_blocks(0, half)):
                row = c * half + index * BLOCK + lax.broadcasted_iota(jnp.int32, (BLOCK, D), 0)
                position = row - 2 * slot + segment * tok
                valid = (row >= 2 * slot) & (position.astype(F32) < length)
                work[block, :] = jnp.where(valid, gb[step, block, :].astype(F32), 0.0)

            @pl.when((c == 0) & (step >= 2))
            def _():
                carry_move(step - 2).wait_recv()
                work[slot : 2 * slot, :] = carb[step - 2]

        sends = []
        for index, (start, size) in enumerate(chunks):
            span = pl.ds(start, size)

            @pl.when(s < last)
            def _():
                handoff(step, index).wait_recv()
                for block in row_blocks(start, size):
                    work[block, :] = gb[step, block, :].astype(F32)

            gain_sum = jnp.zeros((BLOCK // 2, D), F32)
            shift_sum = jnp.zeros((BLOCK // 2, D), F32)
            for block in row_blocks(start, size):
                g = work[block, :]
                z = z2b[side, block, :]
                back = norm_back(g, z, r2b[side, block, :1], gain_two[...])
                dsec[block, :] = back
                dfe[block, :] = back.astype(BF)
                gain_sum += folded_rows(g * z)
                shift_sum += folded_rows(g)
            o_small[2:3, :] += jnp.sum(gain_sum, axis=0, keepdims=True)
            o_small[3:4, :] += jnp.sum(shift_sum, axis=0, keepdims=True)
            if index == 0:
                pl.when(first)(weights[0].wait)
            for lanes in pieces(FF):
                slope = gpb[side, span, lanes].astype(F32)
                pre = (dot(dfe[span], vdown[:, lanes]) * slope).astype(BF)
                dpre[span, lanes] = pre
                row, column = divmod(lanes.start, D)
                o_small[4 + row : 5 + row, column : column + STEP] += jnp.sum(
                    pre.astype(F32), axis=0, keepdims=True
                )
            if index == 0:
                pl.when(first)(weights[1].wait)
            for lanes in pieces(D):
                work[span, lanes] = dsec[span, lanes] + dot(dpre[span], vin[:, lanes])
            gain_sum = jnp.zeros((BLOCK // 2, D), F32)
            shift_sum = jnp.zeros((BLOCK // 2, D), F32)
            for block in row_blocks(start, size):
                g = work[block, :]
                z = z1b[side, block, :]
                back = norm_back(g, z, r1b[side, block, :1], gain_one[...])
                work[block, :] = back
                dbr[block, :] = back.astype(BF)
                gain_sum += folded_rows(g * z)
                shift_sum += folded_rows(g)
            o_small[0:1, :] += jnp.sum(gain_sum, axis=0, keepdims=True)
            o_small[1:2, :] += jnp.sum(shift_sum, axis=0, keepdims=True)
            if index == 0:
                pl.when(first)(weights[2].wait)
            for lanes in pieces(D):
                da[span, lanes] = dot(dbr[span], vproj[:, lanes]).astype(BF)
            for pair in range(PAIRS):
                keys = kvb[side, :, pair_span(pair)]
                values = kvb[side, :, pair_span(pair, D)]
                da2 = stacked_pair(da[span, pair_span(pair)])
                q2 = scaled_queries(qb[side, span, pair_span(pair)])
                dp_ref = dp_tmp.at[pair % 2]
                ds_ref = ds_tmp.at[pair % 2]
                wide = 2 * size
                dp_ref[:, :wide] = dot_nt(values, da2)
                for begin in range(0, wide, 128):
                    lanes = slice(begin, min(begin + 128, wide))
                    kept_lanes = slice(2 * start + begin, 2 * start + lanes.stop)
                    total = jnp.zeros((BLOCK, lanes.stop - begin), F32)
                    for offset in range(0, rows, BLOCK):
                        block = pl.ds(offset, BLOCK)
                        total += probs[side, pair, block, kept_lanes].astype(F32) * dp_ref[block, lanes]
                    total = jnp.sum(total, axis=0, keepdims=True)
                    for offset in range(0, rows, BLOCK):
                        block = pl.ds(offset, BLOCK)
                        ds_ref[block, lanes] = (
                            probs[side, pair, block, kept_lanes].astype(F32) * (dp_ref[block, lanes] - total)
                        ).astype(BF)
                d_keys = dot(ds_ref[:, :wide], q2)
                d_values = dot(probs[side, pair, :, 2 * start : 2 * start + wide], da2)
                if index == 0:
                    dkv[pair, :, :WIDE] = d_keys
                    dkv[pair, :, WIDE:] = d_values
                else:
                    dkv[pair, :, :WIDE] += d_keys
                    dkv[pair, :, WIDE:] += d_values
                if index == len(chunks) - 1:
                    move = remote(
                        dkv.at[pair, theirs],
                        dkv_in.at[side, pair],
                        kv_send.at[pair],
                        kv_recv.at[step, pair],
                        (s, place.other),
                    )
                    move.start()
                    sends.append(move)
                both = dot_tn(keys, ds_ref[:, :wide])
                lane = lax.broadcasted_iota(jnp.int32, (WIDE, size), 0)
                upright = jnp.where(lane < HEAD, both[:, :size], both[:, size:])
                dpj[span, pair_span(pair)] = (jnp.transpose(upright) * HEAD**-0.5).astype(BF)
        pl.when(first)(weights[3].wait)
        for pair in range(PAIRS):
            sends[pair].wait_recv()
            for part in range(2):
                lanes = slice(part * WIDE, (part + 1) * WIDE)
                dpj[:, pair_span(pair, (part + 1) * D)] = (
                    dkv[pair, own, lanes] + dkv_in[side, pair, :, lanes]
                ).astype(BF)
        for index, (start, size) in enumerate(chunks):
            span = pl.ds(start, size)
            for lanes in pieces(D):
                dxb[side, span, lanes] = (
                    work[span, lanes] + dot(dpj[span], vqkv[:, lanes])
                ).astype(BF)
            pl.when(s > 0)(handoff(step, index).start)
            if index == 0:

                @pl.when((s == 0) & (c == 0))
                def _():
                    mgb[step] = dxb[side, :slot].astype(F32) + dxb[side, slot : 2 * slot].astype(F32)
                    pl.when(step < steps - 2)(carry_move(step).start)

        for copy in outgoing(step):
            copy.start()
        outgoing_dx(step).start()
        for move in sends:
            move.wait_send()

        @pl.when(step < steps - 2)
        def _():
            for copy in residuals(step + 2):
                copy.start()

    def one_round(turn, state):
        even, odd = 2 * turn, 2 * turn + 1
        late = (s == last) & (turn == 0)
        prologue(even)
        pl.when(jnp.logical_not(late))(lambda: prologue(odd))
        main(even)
        pl.when(late)(lambda: prologue(odd))
        main(odd)
        return state

    lax.fori_loop(0, segments, one_round, 0)
    settle(steps - 2)
    settle(steps - 1)
    for copy in outgoing(steps - 1):
        copy.wait()

    @pl.when((s == 0) & (c == 0))
    def _():
        for step in range(steps - 2, steps):
            outgoing_memory(step).start()
        for step in range(steps - 2, steps):
            outgoing_memory(step).wait()
        for step in range(steps - 2):
            carry_move(step).wait_send()


def backward(sections, segments, geometry, collective, g0, lens, kept, weights):
    mem, slot, tok, rows = geometry
    half = rows // 2
    steps = 2 * segments

    def grad(width):
        return jax.ShapeDtypeStruct((steps, half, width), BF)

    outs = (
        grad(3 * D),
        grad(D),
        grad(FF),
        grad(D),
        grad(D),
        jax.ShapeDtypeStruct((2, slot, D), F32),
        jax.ShapeDtypeStruct((8, D), F32),
    )
    dma = pltpu.SemaphoreType.DMA
    return pl.pallas_call(
        functools.partial(backward_kernel, sections, segments, geometry),
        name="backward_layer",
        out_shape=outs,
        in_specs=[ANY, VMEM] + [ANY] * 5 + [ANY] * 4 + [VMEM] * 2,
        out_specs=(ANY,) * 6 + (VMEM,),
        scratch_shapes=[
            pltpu.VMEM((3 * D, D), BF),
            pltpu.VMEM((D, D), BF),
            pltpu.VMEM((FF, D), BF),
            pltpu.VMEM((D, FF), BF),
            pltpu.VMEM((steps, half, D), BF),
            pltpu.VMEM((2, half, D), BF),
            pltpu.VMEM((2, rows, 2 * D), BF),
            pltpu.VMEM((2, half, FF), BF),
            pltpu.VMEM((2, half, D), F32),
            pltpu.VMEM((2, half, D), F32),
            pltpu.VMEM((2, half, 128), F32),
            pltpu.VMEM((2, half, 128), F32),
            pltpu.VMEM((2, PAIRS, rows, rows), BF),
            pltpu.VMEM((half, D), F32),
            pltpu.VMEM((half, D), F32),
            pltpu.VMEM((half, D), BF),
            pltpu.VMEM((half, FF), BF),
            pltpu.VMEM((half, D), BF),
            pltpu.VMEM((half, D), BF),
            pltpu.VMEM((2, rows, rows), F32),
            pltpu.VMEM((2, rows, rows), BF),
            pltpu.VMEM((PAIRS, rows, 2 * WIDE), F32),
            pltpu.VMEM((2, PAIRS, half, 2 * WIDE), F32),
            pltpu.VMEM((half, 3 * D), BF),
            pltpu.VMEM((2, half, D), BF),
            pltpu.VMEM((steps, slot, D), F32),
            pltpu.VMEM((steps, slot, D), F32),
            dma((4,)),
            dma((2, 5)),
            dma((steps,)),
            dma((6,)),
            dma((PAIRS,)),
            dma((steps, PAIRS)),
            dma((2, 2)),
            dma((steps, 2)),
            dma((steps,)),
            dma((steps,)),
        ],
        compiler_params=pltpu.CompilerParams(
            collective_id=collective, has_side_effects=True, vmem_limit_bytes=VMEM_LIMIT
        ),
    )(g0, lens, *kept, *weights)


def on_device(
    sections,
    inputs,
    out_grad,
    memory,
    lengths,
    w_qkv,
    w_proj,
    gain_one,
    shift_one,
    w_in,
    b_in,
    w_down,
    gain_two,
    shift_two,
):
    segs, tok, part = inputs.shape[1:]
    mem = memory.shape[1]
    slot = -(-mem // BLOCK) * BLOCK
    rows = -(-(2 * slot + tok) // (2 * BLOCK)) * 2 * BLOCK
    half = rows // 2
    geometry = (mem, slot, tok, rows)
    back_pad = rows - 2 * slot - tok

    def in_slots(array):
        return jnp.pad(array, ((0, 0), (2 * slot, back_pad), (0, 0)))

    def halves(array):
        return array.reshape(segs, 2, half, part).transpose(1, 0, 2, 3)

    tokens = in_slots(inputs[0])
    tokens = tokens.at[0, :mem].set(memory[0]).at[0, slot : slot + mem].set(memory[0])
    cotangent = in_slots(out_grad[0])
    length_tile = jnp.broadcast_to(lengths.astype(F32), (8, 128))
    x_all, g_all, lens = spread(sections, halves(tokens), halves(cotangent), length_tile)

    def by_step(array):
        return array.transpose(2, 0, 3, 1, 4).reshape(2 * segs, half, D)

    matrices = (w_qkv[0], w_proj[0], w_in[0], w_down[0])
    forward_weights = matrices + (gain_one, shift_one, b_in, gain_two, shift_two)
    x, q, kv, att, nb, act, gp, s1, s2, hid, *turned = forward(
        sections, segs, geometry, 2, by_step(x_all), lens, forward_weights
    )
    dpj, dbr, dpre, dfe, dx, memory_term, small = backward(
        sections, segs, geometry, 3, by_step(g_all), lens, (q, kv, gp, s1, s2), (*turned, gain_one, gain_two)
    )

    def per_owner(array):
        return array.reshape(segs, 2, half, sections, part).transpose(1, 3, 0, 2, 4)

    memory_term = memory_term.reshape(2, slot, sections, part).transpose(0, 2, 1, 3)
    out_parts, in_parts, memory_part = collect(sections, per_owner(hid), per_owner(dx), memory_term)

    def owned(parts):
        return parts.transpose(1, 0, 2, 3).reshape(segs, rows, part)[:, 2 * slot : 2 * slot + tok]

    position = jnp.arange(segs * tok, dtype=jnp.int32).reshape(segs, tok)
    token_valid = position < lengths[0]
    outputs = jnp.where(token_valid[:, :, None], owned(out_parts), jnp.zeros((), BF))
    input_grad = owned(in_parts)
    memory_grad = memory_part[:mem]

    def weight_grad(left, right):
        lefts = left.reshape(2 * segs * half, -1)
        rights = right.reshape(2 * segs * half, -1)
        full = jnp.einsum("rd,re->de", lefts, rights, preferred_element_type=F32)
        return lax.psum_scatter(full.astype(BF), "dp", scatter_dimension=0, tiled=True).astype(F32)

    d_qkv = weight_grad(x, dpj)
    d_proj = weight_grad(att, dbr)
    d_in = weight_grad(nb, dpre)
    d_down = weight_grad(act, dfe)
    small = lax.psum(small, "dp")
    devices = lax.axis_size("dp")
    index = lax.axis_index("dp")

    def vector(value):
        size = value.size // devices
        return lax.dynamic_slice_in_dim(value.reshape(-1), index * size, size, 0)[None]

    return (
        outputs[None],
        input_grad[None],
        memory_grad[None],
        d_qkv[None],
        d_proj[None],
        vector(small[0]),
        vector(small[1]),
        d_in[None],
        vector(small[4:8]),
        d_down[None],
        vector(small[2]),
        vector(small[3]),
    )


def solution(mesh):
    return jax.shard_map(
        functools.partial(on_device, mesh.shape["section"]),
        mesh=mesh,
        in_specs=(
            P("dp", None, None, "section"),
            P("dp", None, None, "section"),
            P("dp", None, "section"),
            P("dp"),
            P("section", None, None),
            P("section", None, None),
            P("section", None),
            P("section", None),
            P("section", None, None),
            P("section", None),
            P("section", None, None),
            P("section", None),
            P("section", None),
        ),
        out_specs=(
            P("dp", None, None, "section"),
            P("dp", None, None, "section"),
            P("dp", None, "section"),
            P("section", "dp", None),
            P("section", "dp", None),
            P("section", "dp"),
            P("section", "dp"),
            P("section", "dp", None),
            P("section", "dp"),
            P("section", "dp", None),
            P("section", "dp"),
            P("section", "dp"),
        ),
        check_vma=False,
    )
```

time: 734 us -> 628 us (0.86)
  Pallas kernels: 515 us -> 415 us
  local copies, waits for them, and re-layouts: 50.7 us -> 41.6 us
    pallas_call x4 -> x2, Pallas kernels: 465 us -> 365 us  [the longest x1 259 us: backward(): pl.pallas_call(functools.partial(backward_kernel, sections, segments, geo...]
    another operation x9 -> x1, local copies, waits for them, and re-layouts: 14.5 us -> 0.58 us  [the longest x8 13.9 us: per_owner(): stacked = jnp.stack(arrays, axis=1)]
  transfers between devices with their start and end apart: 4 -> 4, of which waited for: 2 -> 2; matrix products, arithmetic and copies ran while one was open for 8% -> 9% of each run, Pallas kernels for 4% -> 4%
where the time goes in v2:
time: 628 us; the launch traced here: 622 us
  Pallas kernels  415 us (66%)
  waiting for transfers between devices  73 us (12%)
  local copies, waits for them, and re-layouts  41.6 us (7%)
  matrix products  35.7 us (6%)
  blocking collectives  29.5 us (5%)
  between operations  14.9 us (2%)
  other arithmetic  12.2 us (2%)
    pallas_call x1, Pallas kernels, backward(): pl.pallas_call(functools.partial(backward_kernel, sections, segments, geo...  259 us
    pallas_call x1, Pallas kernels, forward(): pl.pallas_call(functools.partial(forward_kernel, sections, segments, geom...  106 us
    reduce_scatter x4, waiting for transfers between devices, weight_grad(): lax.psum_scatter(full.astype(BF), 'dp', scatter_dimension=0, tiled=True)  73 us
    dot_general x4, matrix products, weight_grad(): full = jnp.einsum('rd,re->de', lefts, rights, preferred_element_type=F32)  35.7 us
    psum x1, blocking collectives, on_device(): small = lax.psum(small, 'dp')  29.5 us
    pallas_call x1, Pallas kernels, collect(): pl.pallas_call(functools.partial(collect_kernel, sections), name='collect...  26 us
    pallas_call x1, Pallas kernels, spread(): pl.pallas_call(functools.partial(spread_kernel, sections), name='spread_i...  23.9 us
  transfers between devices with their start and end apart: 4, of which 2 were waited for; matrix products, arithmetic and copies ran while one was open for 9% of the time, Pallas kernels for 4%

profile of v2, /device:TPU:0, one launch (start us, length us, event | category | flops | bytes accessed | tf_op | source)
XLA Modules:
  0.0 622.0 jit_solution(3041033855145057553)
XLA Ops:
  7.2 0.0 copy-start.1
  7.2 0.0 reduce-scatter.7.cloned.1.call-start
  7.2 0.6 fusion.2
  7.8 1.2 copy.29
  9.0 0.1 pad.15
  9.1 1.4 and_reduce_fusion
  10.5 0.8 scatter.6
  11.3 2.7 dynamic-slice_select_fusion
  14.0 1.5 scatter.9
  15.5 0.0 copy-done.1
  15.5 0.2 copy.31
  15.7 0.1 pad.16
  16.4 1.1 copy_bitcast_fusion.2
  17.5 0.6 broadcast_in_dim.59.len_ref
  18.1 23.9 %spread_items.1 = (bf16[2,4,2,272,192]{4,3,2,1,0:T(8,128)(2,1)}, bf16[2,4,2,272,192]{4,3,2,1,0:T(8,128)(2,1)}, f32[2,8,128]{2,1,0:T(8,128)}) custom-call(bf16[2,2,272,192]{3,2,1,0:T(8,128)(2,1)} %get-tuple-element.121.a_ref, bf16[2,2,272,192]{3,2,1,0:T(8,128)(2,1)} %get-tuple-element.120.g_ref, f32[8,128]{1,0:T(8,128)} %broadcast_in_dim.59.len_ref), custom_call_target="tpu_custom_call" | custom-call | tf_op jit(solution)/shard_map/spread_items/pallas_call | solution.py:119
  42.0 3.3 copy.33
  45.4 3.0 reshape.164.x0_ref
  48.4 3.3 copy.35
  51.7 3.0 reshape.166.g0_ref
  54.7 106.0 %forward_layer.1 = (bf16[4,272,768]{2,1,0:T(8,128)(2,1)}, bf16[4,272,768]{2,1,0:T(8,128)(2,1)}, bf16[4,544,1536]{2,1,0:T(8,128)(2,1)}, bf16[4,272,768]{2,1,0:T(8...) custom-call(bf16[4,272,768]{2,1,0:T(8,128)(2,1)} %reshape.164.x0_ref, ...), custom_call_target="tpu_custom_call" | custom-call | tf_op jit(solution)/shard_map/forward_layer/pallas_call | solution.py:581
  160.8 258.9 %backward_layer.1 = (bf16[4,272,2304]{2,1,0:T(8,128)(2,1)}, bf16[4,272,768]{2,1,0:T(8,128)(2,1)}, bf16[4,272,3072]{2,1,0:T(8,128)(2,1)}, bf16[4,272,768]{2,1,0:T...) custom-call(bf16[4,272,768]{2,1,0:T(8,128)(2,1)} %reshape.166.g0_ref, ...), custom_call_target="tpu_custom_call" | custom-call | tf_op jit(solution)/shard_map/backward_layer/pallas_call | solution.py:1007
  419.7 0.0 copy-start.7
  419.7 4.8 bitcast_convert_fusion.3
  424.5 0.0 reduce-scatter.7.cloned.1.call-update
  424.5 0.0 reduce-scatter.5.cloned.1.call-start
  424.6 0.0 copy-done.7
  424.6 8.7 %bitcast_convert_fusion.2 = bf16[768,2304]{1,0:T(8,128)(2,1)} fusion(bf16[4,272,768]{2,1,0:T(8,128)(2,1)S(1)} %copy-done.7, bf16[4,272,2304]{2,1,0:T(8,128)(2,1)} %get-tuple-element.82), kind=kOutput, calls=%fused_computation.2 | convolution fusion | flops 3852140544 | bytes 10223616 | tf_op jit(solution)/shard_map/rd,re->de/dot_general | solution.py:1124
  433.3 0.0 reduce-scatter.5.cloned.1.call-update
  433.3 0.0 reduce-scatter.11.cloned.1.call-start
  433.4 1.4 copy-done.6
  434.7 11.1 %bitcast_convert_fusion = bf16[3072,768]{1,0:T(8,128)(2,1)} fusion(bf16[4,272,3072]{2,1,0:T(8,128)(2,1)} %get-tuple-element.88, bf16[4,272,768]{2,1,0:T(8,128)(2,1)S(1)} %copy-done.6), kind=kOutput, calls=%fused_computation | convolution fusion | flops 5136187392 | bytes 13074432 | tf_op jit(solution)/shard_map/rd,re->de/dot_general | solution.py:1124
  445.9 0.0 reduce-scatter.11.cloned.1.call-update
  445.9 0.0 reduce-scatter.9.cloned.1.call-start
  445.9 1.4 copy-done.5
  447.3 11.1 %bitcast_convert_fusion.1 = bf16[768,3072]{1,0:T(8,128)(2,1)} fusion(bf16[4,272,768]{2,1,0:T(8,128)(2,1)S(1)} %copy-done.5, bf16[4,272,3072]{2,1,0:T(8,128)(2,1)} %get-tuple-element.87), kind=kOutput, calls=%fused_computation.1 | convolution fusion | flops 5136187392 | bytes 13074432 | tf_op jit(solution)/shard_map/rd,re->de/dot_general | solution.py:1124
  458.4 0.0 reduce-scatter.9.cloned.1.call-update
  458.4 4.6 reshape.167
  463.0 0.0 copy-start.2
  463.0 1.7 copy.48
  464.7 0.0 copy-done.2
  464.7 0.1 reshape.168
  464.8 0.7 copy.50
  465.5 4.6 reshape.165
  470.1 1.7 copy.49
  471.8 26.0 %collect_results.1 = (bf16[2,2,272,192]{3,2,1,0:T(8,128)(2,1)}, bf16[2,2,272,192]{3,2,1,0:T(8,128)(2,1)}, f32[16,192]{1,0:T(8,128)}) custom-call(bf16[2,4,2,272,192]{4,3,2,1,0:T(8,128)(2,1)} %bitcast.67, bf16[2,4,2,272,192]{4,3,2,1,0:T(8,128)(2,1)} %bitcast.66, f32[2,4,16,192]{3,2,1,0:T(8,128)} %bitcast.82), custom_call_target="tpu_custom_call" | custom-call | tf_op jit(solution)/shard_map/collect_results/pallas_call | solution.py:207
  497.8 0.0 copy-start
  497.8 1.1 copy.38
  498.9 0.2 fusion
  499.2 0.9 copy.40
  500.2 0.9 copy.41
  501.1 0.6 copy.42
  501.8 29.5 %psum.7 = f32[8,768]{1,0:T(8,128)S(1)} all-reduce(f32[8,768]{1,0:T(8,128)S(1)} %copy-done.3), channel_id=1, replica_groups=mesh['section'=4,'dp'=8] {'dp'}, use_global_device_ids=true, to_apply=%region_3.4 | all-reduce | flops 6144 | bytes 49152 | tf_op jit(solution)/shard_map/psum | solution.py:1131
  531.3 0.1 dynamic_slice.17
  531.4 0.6 broadcast_in_dim.70
  532.0 0.6 constant_dynamic-slice_fusion
  532.6 0.6 constant_dynamic-slice_fusion.1
  533.1 0.6 constant_dynamic-slice_fusion.2
  533.7 0.6 constant_dynamic-slice_fusion.3
  534.3 1.6 bitcast_convert_fusion.7
  535.9 2.0 bitcast_convert_fusion.6
  537.9 19.6 %reduce-scatter.11.cloned.1.call-done = bf16[384,768]{1,0:T(8,128)(2,1)} async-done(((bf16[3072,768]{1,0:T(8,128)(2,1)}), bf16[384,768]{1,0:T(8,128)(2,1)}) %reduce-scatter.11.cloned.1.call-update) | async-done | bytes 589840 | tf_op jit(solution)/shard_map/reduce_scatter | solution.py:1125
  557.6 2.2 bitcast_convert_fusion.4
  559.7 53.3 %reduce-scatter.9.cloned.1.call-done = bf16[96,3072]{1,0:T(8,128)(2,1)} async-done(((bf16[768,3072]{1,0:T(8,128)(2,1)}), bf16[96,3072]{1,0:T(8,128)(2,1)}) %reduce-scatter.9.cloned.1.call-update) | async-done | bytes 589840 | tf_op jit(solution)/shard_map/reduce_scatter | solution.py:1125
  613.0 2.2 bitcast_convert_fusion.5
  (17 shorter events, 0.1 us)
Async XLA Ops:
  7.2 8.3 %copy-start.1 = (bf16[1,2,502,192]{2,3,1,0:T(8,128)(2,1)S(1)}, bf16[1,2,502,192]{2,3,1,0:T(8,128)(2,1)}, u32[]{:S(2)}) copy-start(bf16[1,2,502,192]{2,3,1,0:T(8,128)(2,1)} %param.18) | copy-start | bytes 1156612
  7.2 527.1 %reduce-scatter.7.cloned.1.call-start = ((), (), s32[]{:S(2)}) async-start(), calls=%async_computation.5 | async-start | bytes 1327104 | tf_op jit(solution)/shard_map/reduce_scatter | solution.py:1125
  419.7 4.9 copy-start.7
  424.5 111.4 %reduce-scatter.5.cloned.1.call-start = ((), (), s32[]{:S(2)}) async-start(), calls=%async_computation.4 | async-start | bytes 3981312 | tf_op jit(solution)/shard_map/reduce_scatter | solution.py:1125
  433.3 1.4 copy-start.6
  433.3 124.2 %reduce-scatter.11.cloned.1.call-start = ((), (), s32[]{:S(2)}) async-start(), calls=%async_computation.7 | async-start | bytes 5308416 | tf_op jit(solution)/shard_map/reduce_scatter | solution.py:1125
  445.9 1.4 copy-start.5
  445.9 167.1 %reduce-scatter.9.cloned.1.call-start = ((), (), s32[]{:S(2)}) async-start(), calls=%async_computation.6 | async-start | bytes 5308416 | tf_op jit(solution)/shard_map/reduce_scatter | solution.py:1125
  463.0 1.7 copy-start.2
  497.8 2.3 copy-start
  499.1 2.0 copy-start.4
  499.2 2.6 copy-start.3
Sparse Core Ops, SparseCore 0:
  424.7 32.0 reduce-scatter.6
  459.0 42.1 reduce-scatter.4
  503.6 53.9 reduce-scatter.10
  559.8 53.1 reduce-scatter.8
